TPU v7x, 32 devices: a whole 2x2x4 slice. The times are simulated.
32 devices in a mesh: tile: 32 (over z, y, x, core).
Axes of the slice: x: 2, y: 2, z: 4, core: 2. Of those that a mesh axis runs over, the one named last changes fastest.
Arguments:
- adjoint_zonal: bfloat16 [32, 8, 512, 128], P(None, None, 'tile'), may hold values from -70 to 70
- adjoint_meridional: bfloat16 [32, 8, 512, 128], P(None, None, 'tile'), may hold values from -70 to 70
- cell_fraction: bfloat16 [8, 512, 128], P(None, 'tile'), may hold values from 0.19921875 to 1
- level_thickness: float32 [8], replicated, may hold values from 0.5 to 2
- land_mask: int32 [512, 128], P('tile'), may hold values 0 or 1
- edge_codes: int32 [32, 4], P('tile'), may hold values from 0 to 1, as said below
Outputs:
- surface_adjoint: float32 [32, 512, 128], P(None, 'tile')
- residual: float32 [32, 512, 128], P(None, 'tile')
Inputs may be any that keep to these rules, and one draw needn't show every extreme that they name: edge_codes[t, 1] equals edge_codes[t - 1, 0] and edge_codes[t, 3] equals edge_codes[t - 16, 2], tile numbers taken modulo 32.
All inputs are finite; a program needn't handle non-finite values. No bound on the sum of `land_mask` on one device may be relied on, other than what follows from the above.
Results may differ from a plain program's by a relative error of at most 0.0003.
Values may be sent and summed in bfloat16 or wider, within the bound.
No kernel may reach another device: no remote copies, remote signals or barrier semaphores. Data moves between devices by JAX's collectives and lax.ppermute only.
A program may use at most 64 MiB of HBM per device.

v0:
```python
import functools

import jax
import jax.numpy as jnp
from jax import lax
from jax.experimental import pallas as pl
from jax.experimental.pallas import tpu as pltpu
from jax.sharding import PartitionSpec as P

NTX = 16
ITERS = 4
CHUNK = 32
EXTRA = 8
LIMIT = 56 * 1024 * 1024

coupling_coef = 0.25


def column_depth(fraction, thickness, wet_cells):
    running = thickness[0] * fraction[0].astype(jnp.float32)
    for level in range(1, fraction.shape[0]):
        running = running + thickness[level] * fraction[level].astype(jnp.float32)
    return wet_cells * running


def message_kernel(thickness_ref, codes_ref, zonal_ref, meridional_ref, fraction_ref, out_ref):
    members, levels, rows, columns = zonal_ref.shape
    lane = lax.broadcasted_iota(jnp.int32, (rows, columns), 1)
    row = lax.broadcasted_iota(jnp.int32, (rows, columns), 0)
    place = lax.broadcasted_iota(jnp.int32, (EXTRA, columns), 0)
    wide = lax.broadcasted_iota(jnp.int32, (EXTRA, columns), 1)
    code = [jnp.where(codes_ref[0, side] == 1, 1.0, 0.0) for side in range(4)]
    flags = jnp.where(place == 2, jnp.where(wide >= columns // 2, code[0], code[1]), 0.0)
    flags = jnp.where(place == 3, code[2], jnp.where(place == 4, code[3], flags))
    parts = [
        thickness_ref[level] * fraction_ref[level].astype(jnp.float32) for level in range(levels)
    ]
    for member in range(members):
        along = parts[0] * zonal_ref[member, 0].astype(jnp.float32)
        across = parts[0] * meridional_ref[member, 0].astype(jnp.float32)
        for level in range(1, levels):
            along = along + parts[level] * zonal_ref[member, level].astype(jnp.float32)
            across = across + parts[level] * meridional_ref[member, level].astype(jnp.float32)
        east = jnp.where(lane == columns - 1, 0.0, pltpu.roll(along, columns - 1, 1))
        north = jnp.where(row == rows - 1, 0.0, pltpu.roll(across, rows - 1, 0))
        out_ref[member, 0:rows] = along - east + across - north
        first = jnp.where(lane == row, along[:, 0:1], 0.0)
        first = jnp.sum(first, axis=0, keepdims=True)
        out_ref[member, rows : rows + EXTRA] = jnp.where(
            place == 0, across[0:1], jnp.where(place == 1, first, flags)
        )


def message_of(zonal, meridional, fraction, thickness, codes):
    members, levels, rows, columns = zonal.shape
    step = 8 if members % 8 == 0 else 1
    field = pl.BlockSpec((step, levels, rows, columns), lambda at: (at, 0, 0, 0))
    return pl.pallas_call(
        message_kernel,
        grid=(members // step,),
        in_specs=[
            pl.BlockSpec(memory_space=pltpu.SMEM),
            pl.BlockSpec(memory_space=pltpu.SMEM),
            field,
            field,
            pl.BlockSpec((levels, rows, columns), lambda at: (0, 0, 0)),
        ],
        out_specs=pl.BlockSpec((step, rows + EXTRA, columns), lambda at: (at, 0, 0)),
        out_shape=jax.ShapeDtypeStruct((members, rows + EXTRA, columns), jnp.float32),
        compiler_params=pltpu.CompilerParams(vmem_limit_bytes=LIMIT),
    )(thickness, codes, zonal, meridional, fraction)


def reversed_rows(values):
    groups = values.shape[0] // 8
    index = 7 - lax.broadcasted_iota(jnp.int32, (8, values.shape[1]), 0)
    pieces = [
        jnp.take_along_axis(
            values[8 * at : 8 * at + 8], index, axis=0, mode="promise_in_bounds"
        )
        for at in reversed(range(groups))
    ]
    return jnp.concatenate(pieces, axis=0)


def reversed_lanes(values):
    columns = values.shape[1]
    index = columns - 1 - lax.broadcasted_iota(jnp.int32, values.shape, 1)
    return jnp.take_along_axis(values, index, axis=1, mode="promise_in_bounds")


def cg_kernel(
    got_ref, depth_ref, out_ref, direction_ref, image_ref, east_ref, west_ref, north_ref, south_ref, total_ref
):
    tiles, rows, columns = depth_ref.shape
    lane = lax.broadcasted_iota(jnp.int32, (rows, columns), 1)
    row = lax.broadcasted_iota(jnp.int32, (rows, columns), 0)
    near = lax.broadcasted_iota(jnp.int32, (8, columns), 0)
    chunk = min(CHUNK, tiles)

    def over_tiles(body, carry):
        if tiles == chunk:
            for tile in range(tiles):
                carry = body(tile, carry)
            return carry

        def some(at, inner):
            for tile in range(chunk):
                inner = body(at * chunk + tile, inner)
            return inner

        return lax.fori_loop(0, tiles // chunk, some, carry)

    def shift(tile, by):
        if isinstance(tile, int):
            return (tile + by) % tiles
        return lax.rem(tile + by + tiles, tiles)

    def neighbours(ref, tile):
        own = ref[tile]
        flip_sides = got_ref[tile, rows + 2 : rows + 3, :] > 0.5
        side = jnp.where(
            lane == columns - 1,
            pltpu.roll(ref[shift(tile, 1)], columns - 1, 1),
            pltpu.roll(ref[shift(tile, -1)], 1, 1),
        )
        side = jnp.where(flip_sides, reversed_rows(side), side)
        east = jnp.where(lane == columns - 1, side, pltpu.roll(own, columns - 1, 1))
        west = jnp.where(lane == 0, side, pltpu.roll(own, 1, 1))
        flip_ends = (
            jnp.where(
                near == 7,
                got_ref[tile, rows + 3 : rows + 4, :],
                got_ref[tile, rows + 4 : rows + 5, :],
            )
            > 0.5
        )
        ends = jnp.where(
            near == 7,
            ref[shift(tile, NTX), 0:1, :],
            ref[shift(tile, -NTX), rows - 1 : rows, :],
        )
        ends = jnp.where(flip_ends, reversed_lanes(ends), ends)
        ends = jnp.concatenate([ends] * (rows // 8), axis=0)
        north = jnp.where(row == rows - 1, ends, pltpu.roll(own, rows - 1, 0))
        south = jnp.where(row == 0, ends, pltpu.roll(own, 1, 0))
        return own, east, west, north, south

    def prepare(tile, carry):
        image_ref[tile] = jnp.sqrt(depth_ref[tile])
        return carry

    over_tiles(prepare, 0)

    def begin(tile, norm):
        own, east, west, north, south = neighbours(image_ref, tile)
        scaled = coupling_coef * own
        east, west, north, south = scaled * east, scaled * west, scaled * north, scaled * south
        east_ref[tile], west_ref[tile], north_ref[tile], south_ref[tile] = east, west, north, south
        total_ref[tile] = 1.0 + ((east + west) + (north + south))
        flip_east = got_ref[tile, rows + 2 : rows + 3, columns - 1 : columns] > 0.5
        target = jnp.where(flip_east, rows - 1 - row, row)
        edge = jnp.where(lane == target, got_ref[shift(tile, 1), rows + 1 : rows + 2, :], 0.0)
        edge = jnp.sum(edge, axis=1, keepdims=True)
        flip_north = got_ref[tile, rows + 3 : rows + 4, :] > 0.5
        end = jnp.broadcast_to(got_ref[shift(tile, NTX), rows : rows + 1, :], (8, columns))
        end = jnp.where(flip_north, reversed_lanes(end), end)
        end = jnp.concatenate([end] * (rows // 8), axis=0)
        field = got_ref[tile, 0:rows]
        field = field - jnp.where(lane == columns - 1, edge, 0.0)
        field = field - jnp.where(row == rows - 1, end, 0.0)
        field = jnp.where(depth_ref[tile] > 0.0, field, 0.0)
        out_ref[tile, rows : 2 * rows] = field
        direction_ref[tile] = field
        out_ref[tile, 0:rows] = jnp.zeros_like(field)
        return norm + field * field

    def all_of(total):
        return jnp.sum(total, keepdims=True)

    zero = jnp.zeros((rows, columns), jnp.float32)

    def iteration(_, norm):
        def apply(tile, total):
            own, east, west, north, south = neighbours(direction_ref, tile)
            image = total_ref[tile] * own - (
                (east_ref[tile] * east + west_ref[tile] * west)
                + (north_ref[tile] * north + south_ref[tile] * south)
            )
            image_ref[tile] = image
            return total + own * image

        step = norm / all_of(over_tiles(apply, zero))

        def advance(tile, total):
            out_ref[tile, 0:rows] = out_ref[tile, 0:rows] + step * direction_ref[tile]
            residual = out_ref[tile, rows : 2 * rows] - step * image_ref[tile]
            out_ref[tile, rows : 2 * rows] = residual
            return total + residual * residual

        later = all_of(over_tiles(advance, zero))
        ratio = later / norm

        def turn(tile, carry):
            direction_ref[tile] = out_ref[tile, rows : 2 * rows] + ratio * direction_ref[tile]
            return carry

        over_tiles(turn, 0)
        return later

    lax.fori_loop(0, ITERS, iteration, all_of(over_tiles(begin, zero)))


def cg_of(got, depth):
    tiles, rows, columns = depth.shape
    field = pltpu.VMEM((tiles, rows, columns), jnp.float32)
    return pl.pallas_call(
        cg_kernel,
        in_specs=[pl.BlockSpec(memory_space=pltpu.VMEM)] * 2,
        out_specs=pl.BlockSpec(memory_space=pltpu.VMEM),
        out_shape=jax.ShapeDtypeStruct((tiles, 2 * rows, columns), jnp.float32),
        scratch_shapes=[field] * 7,
        compiler_params=pltpu.CompilerParams(vmem_limit_bytes=LIMIT),
    )(got, depth)


def on_device(zonal, meridional, fraction, thickness, land_mask, edge_codes):
    tiles = lax.axis_size("tile")
    members, _, rows, columns = zonal.shape
    depth = column_depth(fraction, thickness, land_mask.astype(jnp.float32))
    depth = lax.all_gather(depth, "tile")
    message = message_of(zonal, meridional, fraction, thickness, edge_codes)
    if tiles > members:
        message = jnp.pad(message, ((0, tiles - members), (0, 0), (0, 0)))
    got = lax.all_to_all(message, "tile", split_axis=0, concat_axis=0, tiled=True)
    back = cg_of(got, depth)
    home = lax.all_to_all(back, "tile", split_axis=0, concat_axis=0, tiled=True)[:members]
    return home[:, :rows], home[:, rows:]


def solution(mesh):
    in_specs = (
        P(None, None, "tile", None),
        P(None, None, "tile", None),
        P(None, "tile", None),
        P(),
        P("tile", None),
        P("tile", None),
    )
    out_specs = (P(None, "tile", None), P(None, "tile", None))
    return jax.shard_map(
        on_device, mesh=mesh, in_specs=in_specs, out_specs=out_specs, check_vma=False
    )
```

profile of v0, /device:TPU:0, one launch (start us, length us, event | category | flops | bytes accessed | tf_op | source)
XLA Modules:
  0.0 90.4 jit_solution(2096497912612705209)
XLA Ops:
  0.6 3.7 %shard_map.77 = f32[32,24,128]{2,1,0:T(8,128)} custom-call(f32[8]{0:T(128)} %thickness_ref.1, s32[1,4]{1,0:T(1,128)} %codes_ref.1, bf16[32,8,16,128]{3,2,1,0:T(8,128)(2,1)} %zonal_ref.1, bf16[32,8,16,128]{3,2,1,0:T(8,128)(2,1)} %meridional_ref.1, bf16[8,16,128]{2,1,0:T(8,128)(2,1)} %fraction_ref.1), custom_call_target="tpu_custom_call" | custom-call | tf_op jit(solution)/shard_map/pallas_call | solution.py:58
  4.3 0.0 copy-start.2
  4.3 0.0 copy-start.3
  4.3 7.3 %all-to-all-start = ((f32[32,24,128]{2,1,0:T(8,128)}), f32[32,24,128]{2,1,0:T(8,128)S(1)}, u32[]{:S(2)}, u32[]{:S(2)}) async-start(f32[32,24,128]{2,1,0:T(8,128)} %shard_map.77), calls=%async_computation | async-start | bytes 786432 | tf_op jit(solution)/shard_map/all_to_all | solution.py:235
  11.6 0.0 copy-done.2
  11.6 0.0 copy-start.1
  11.7 0.7 fusion.1
  12.3 0.0 copy-done.3
  12.3 0.1 copy-done.1
  12.4 5.0 %bitcast_multiply_fusion = f32[16,128]{1,0:T(8,128)S(1)} fusion(s32[16,128]{1,0:T(8,128)S(1)} %copy-done.3, bf16[8,16,128]{2,1,0:T(8,128)(2,1)S(1)} %copy-done.1, f32[]{:T(128)} %bitcast.7, f32[]{:T(128)} %bitcast.6, f32[]{:T(128)} %bitcast.5, f32[]{:T(128)} %bitcast.4, f32[]{:T(128)} %bitcast.3, f32[]{:T(128)} %bitcast.2, f32[]{:T(128)} %bitcast.1, f32[]{:T(128)} %bitcast), kind=kLoop, calls=%fused_computation | loop fusion | flops 51200 | bytes 49184 | tf_op jit(solution)/shard_map/mul | solution.py:23
  17.4 45.1 %all-gather = f32[512,128]{1,0:T(8,128)} all-gather(f32[16,128]{1,0:T(8,128)S(1)} %bitcast_multiply_fusion), channel_id=2, replica_groups=mesh['tile'=32] {'tile'}, dimensions={0}, use_global_device_ids=true | all-gather | bytes 270336 | tf_op jit(solution)/shard_map/all_gather | solution.py:231
  62.6 0.0 all-to-all-done.got_ref
  62.6 0.0 copy-start
  62.6 0.8 copy-done
  63.3 8.1 %shard_map.78 = f32[32,32,128]{2,1,0:T(8,128)} custom-call(f32[32,24,128]{2,1,0:T(8,128)} %copy-done, f32[32,16,128]{2,1,0:T(8,128)} %bitcast.11), custom_call_target="tpu_custom_call" | custom-call | tf_op jit(solution)/shard_map/pallas_call | solution.py:217
  71.4 18.1 %all_to_all.10 = f32[32,32,128]{2,1,0:T(8,128)S(1)} all-to-all(f32[32,32,128]{2,1,0:T(8,128)} %shard_map.78), channel_id=1, replica_groups=mesh['tile'=32] {'tile'}, dimensions={0} | all-to-all | bytes 1048576 | tf_op jit(solution)/shard_map/all_to_all | solution.py:237
  89.6 0.8 fusion
Async XLA Ops:
  4.3 7.3 %copy-start.2 = (f32[8]{0:T(128)S(1)}, f32[8]{0:T(128)}, u32[]{:S(2)}) copy-start(f32[8]{0:T(128)} %thickness_ref.1) | copy-start | bytes 100
  4.3 8.0 %copy-start.3 = (s32[16,128]{1,0:T(8,128)S(1)}, s32[16,128]{1,0:T(8,128)}, u32[]{:S(2)}) copy-start(s32[16,128]{1,0:T(8,128)} %param.10) | copy-start | bytes 24580
  4.3 58.3 %all-to-all-start = ((f32[32,24,128]{2,1,0:T(8,128)}), f32[32,24,128]{2,1,0:T(8,128)S(1)}, u32[]{:S(2)}, u32[]{:S(2)}) async-start(f32[32,24,128]{2,1,0:T(8,128)} %shard_map.77), calls=%async_computation | async-start | bytes 786432 | tf_op jit(solution)/shard_map/all_to_all | solution.py:235
  11.6 0.8 copy-start.1
  62.6 0.8 copy-start
where the time goes:
time: 90.9 us; the launch traced here: 90.4 us
  blocking collectives  63.3 us (70%)
  Pallas kernels  11.8 us (13%)
  starting transfers between devices  7.3 us (8%)
  other arithmetic  5.03 us (6%)
  local copies, waits for them, and re-layouts  2.34 us (3%)
    all_gather x1, blocking collectives, on_device(): depth = lax.all_gather(depth, 'tile')  45.1 us
    all_to_all x1, blocking collectives, on_device(): lax.all_to_all(back, 'tile', split_axis=0, concat_axis=0, tiled=True)  18.1 us
    pallas_call x1, Pallas kernels, cg_of(): pl.pallas_call(cg_kernel, in_specs=[pl.BlockSpec(memory_space=pltpu.VMEM)...  8.07 us
    all_to_all x1, starting transfers between devices, on_device(): lax.all_to_all(message, 'tile', split_axis=0, concat_axis=0, tiled=True)  7.3 us
    mul x1, other arithmetic, column_depth(): return wet_cells * running  5.03 us
    pallas_call x1, Pallas kernels, message_of(): pl.pallas_call(message_kernel, grid=(members // step,), in_specs=[pl.Bloc...  3.69 us
  transfers between devices with their start and end apart: 1, of which 0 were waited for; matrix products, arithmetic and copies ran while one was open for 6% of the time, Pallas kernels for 0%

commit v1 on v0

v1 whole, which is shorter than its diff:
```python
import functools

import jax
import jax.numpy as jnp
from jax import lax
from jax.experimental import pallas as pl
from jax.experimental.pallas import tpu as pltpu
from jax.sharding import PartitionSpec as P

NTX = 16
ITERS = 4
CHUNK = 32
STEPS = 262143.0
LIMIT = 56 * 1024 * 1024

coupling_coef = 0.25


def message_kernel(
    thickness_ref, codes_ref, zonal_ref, meridional_ref, fraction_ref, land_ref, out_ref
):
    members, levels, rows, columns = zonal_ref.shape
    lane = lax.broadcasted_iota(jnp.int32, (rows, columns), 1)
    row = lax.broadcasted_iota(jnp.int32, (rows, columns), 0)
    place = lax.broadcasted_iota(jnp.int32, (8, columns), 0)
    wide = lax.broadcasted_iota(jnp.int32, (8, columns), 1)
    code = [jnp.where(codes_ref[0, side] == 1, 1.0, 0.0) for side in range(4)]
    parts = [
        thickness_ref[level] * fraction_ref[level].astype(jnp.float32) for level in range(levels)
    ]
    depth = functools.reduce(lambda one, other: one + other, parts)
    whole = sum_of(thickness_ref, levels)
    steps = jnp.floor(jnp.where(land_ref[...] == 1, depth * (STEPS / whole), 0.0) + 0.5)
    upper, lower = steps[0:8], steps[8:16]
    high = jnp.floor(lower * (1.0 / 64.0))
    words = upper + 262144.0 * (lower - 64.0 * high)
    rest = high + 4096.0 * pltpu.roll(high, 4, 0)
    rest = jnp.where(place == 6, jnp.where(wide >= columns // 2, code[0], code[1]), rest)
    rest = jnp.where(place == 7, code[2] + 2.0 * code[3], rest)
    for member in range(members):
        along = parts[0] * zonal_ref[member, 0].astype(jnp.float32)
        across = parts[0] * meridional_ref[member, 0].astype(jnp.float32)
        for level in range(1, levels):
            along = along + parts[level] * zonal_ref[member, level].astype(jnp.float32)
            across = across + parts[level] * meridional_ref[member, level].astype(jnp.float32)
        east = jnp.where(lane == columns - 1, 0.0, pltpu.roll(along, columns - 1, 1))
        north = jnp.where(row == rows - 1, 0.0, pltpu.roll(across, rows - 1, 0))
        out_ref[member, 0:rows] = along - east + across - north
        first = jnp.where(lane == row, along[:, 0:1], 0.0)
        first = jnp.sum(first, axis=0, keepdims=True)
        out_ref[member, rows : rows + 8] = words
        out_ref[member, rows + 8 : rows + 16] = jnp.where(
            place == 4, across[0:1], jnp.where(place == 5, first, rest)
        )


def sum_of(thickness_ref, levels):
    whole = thickness_ref[0]
    for level in range(1, levels):
        whole = whole + thickness_ref[level]
    return whole


def message_of(zonal, meridional, fraction, thickness, land_mask, codes):
    members, levels, rows, columns = zonal.shape
    step = 8 if members % 8 == 0 else 1
    field = pl.BlockSpec((step, levels, rows, columns), lambda at: (at, 0, 0, 0))
    return pl.pallas_call(
        message_kernel,
        grid=(members // step,),
        in_specs=[
            pl.BlockSpec(memory_space=pltpu.SMEM),
            pl.BlockSpec(memory_space=pltpu.SMEM),
            field,
            field,
            pl.BlockSpec((levels, rows, columns), lambda at: (0, 0, 0)),
            pl.BlockSpec((rows, columns), lambda at: (0, 0)),
        ],
        out_specs=pl.BlockSpec((step, 2 * rows, columns), lambda at: (at, 0, 0)),
        out_shape=jax.ShapeDtypeStruct((members, 2 * rows, columns), jnp.float32),
        compiler_params=pltpu.CompilerParams(vmem_limit_bytes=LIMIT),
    )(thickness, codes, zonal, meridional, fraction, land_mask)


def reversed_rows(values):
    groups = values.shape[0] // 8
    index = 7 - lax.broadcasted_iota(jnp.int32, (8, values.shape[1]), 0)
    pieces = [
        jnp.take_along_axis(
            values[8 * at : 8 * at + 8], index, axis=0, mode="promise_in_bounds"
        )
        for at in reversed(range(groups))
    ]
    return jnp.concatenate(pieces, axis=0)


def reversed_lanes(values):
    columns = values.shape[1]
    index = columns - 1 - lax.broadcasted_iota(jnp.int32, values.shape, 1)
    return jnp.take_along_axis(values, index, axis=1, mode="promise_in_bounds")


def cg_kernel(
    thickness_ref,
    got_ref,
    out_ref,
    field_ref,
    image_ref,
    east_ref,
    west_ref,
    north_ref,
    south_ref,
    total_ref,
    side_ref,
    turned_ref,
    ends_ref,
):
    tiles, rows, columns = image_ref.shape
    levels = thickness_ref.shape[0]
    lane = lax.broadcasted_iota(jnp.int32, (rows, columns), 1)
    row = lax.broadcasted_iota(jnp.int32, (rows, columns), 0)
    near = lax.broadcasted_iota(jnp.int32, (8, columns), 0)
    chunk = min(CHUNK, tiles)

    def over_tiles(body, carry):
        def some(base, inner):
            rolled = {}
            for step in range(chunk):
                inner = body(base, step, rolled, inner)
            return inner

        if tiles == chunk:
            return some(0, carry)
        return lax.fori_loop(0, tiles // chunk, lambda at, inner: some(at * chunk, inner), carry)

    def shift(base, by):
        if isinstance(base, int):
            return (base + by) % tiles
        return lax.rem(base + by + tiles, tiles)

    def first_row(tile):
        at = tile * rows + 8
        return at if isinstance(at, int) else pl.multiple_of(at, 8)

    def field(tile, by=0):
        return field_ref[pl.ds(first_row(tile) + by, rows), :]

    def turned(base, step, rolled, by):
        key = (step, by)
        if key not in rolled:
            rolled[key] = pltpu.roll(field(shift(base, step)), by, 1)
        return rolled[key]

    def flip_sides(tile):
        return got_ref[tile, 2 * rows - 2 : 2 * rows - 1, :] > 0.5

    def flip_ends(tile):
        both = got_ref[tile, 2 * rows - 1 : 2 * rows, :]
        south = jnp.where(both > 1.5, 1.0, 0.0)
        return jnp.where(near == 7, both - 2.0 * south, south) > 0.5

    def neighbours(base, step, rolled):
        tile = shift(base, step)
        own = field(tile)
        east = turned(base, step, rolled, columns - 1)
        west = turned(base, step, rolled, 1)
        side = jnp.where(
            lane >= columns // 2,
            turned(base, step + 1, rolled, columns - 1),
            turned(base, step - 1, rolled, 1),
        )
        ends = jnp.where(
            near == 7,
            field_ref[pl.ds(first_row(shift(base, step + NTX)), 1), :],
            field_ref[pl.ds(first_row(shift(base, step - NTX)) + rows - 1, 1), :],
        )
        ends = jnp.where(flip_ends(tile), reversed_lanes(ends), ends)
        return own, east, west, field(tile, 1), field(tile, -1), side, reversed_rows(side), ends

    levels_sum = sum_of(thickness_ref, levels)
    padding = jnp.zeros((8, columns), jnp.float32)
    field_ref[0:8, :] = padding
    field_ref[tiles * rows + 8 : tiles * rows + 16, :] = padding

    def read_depth(base, step, rolled, carry):
        tile = shift(base, step)
        words = got_ref[tile, rows : rows + 8, :]
        rest = got_ref[tile, rows + 8 : rows + 16, :]
        low = jnp.floor(words * (1.0 / 262144.0))
        upper = words - 262144.0 * low
        second = jnp.floor(rest * (1.0 / 4096.0))
        high = jnp.where(near < 4, rest - 4096.0 * second, pltpu.roll(second, 4, 0))
        lower = low + 64.0 * high
        depth = jnp.concatenate([upper, lower], axis=0) * (levels_sum / STEPS)
        field_ref[pl.ds(first_row(tile), rows), :] = jnp.sqrt(depth)
        return carry

    over_tiles(read_depth, 0)

    def weights(base, step, rolled, carry):
        tile = shift(base, step)
        own, east, west, north, south, side, side_turned, ends = neighbours(base, step, rolled)
        own = coupling_coef * own
        east = jnp.where(lane == columns - 1, 0.0, own * east)
        west = jnp.where(lane == 0, 0.0, own * west)
        north = jnp.where(row == rows - 1, 0.0, own * north)
        south = jnp.where(row == 0, 0.0, own * south)
        edge = jnp.logical_or(lane == 0, lane == columns - 1)
        side = jnp.where(edge, own * jnp.where(flip_sides(tile), side_turned, side), 0.0)
        upper = jnp.where(near == 0, own[0:8] * ends, 0.0)
        lower = jnp.where(near == 7, own[rows - 8 : rows] * ends, 0.0)
        east_ref[tile], west_ref[tile], north_ref[tile], south_ref[tile] = east, west, north, south
        side_ref[tile] = jnp.where(flip_sides(tile), 0.0, side)
        turned_ref[tile] = jnp.where(flip_sides(tile), side, 0.0)
        both = jnp.concatenate([upper, lower], axis=0)
        ends_ref[tile] = both
        total_ref[tile] = 1.0 + ((east + west) + (north + south)) + (side + both)
        return carry

    over_tiles(weights, 0)

    def begin(base, step, rolled, norm):
        tile = shift(base, step)
        wet = field(tile) > 0.0
        flip_east = got_ref[tile, 2 * rows - 2 : 2 * rows - 1, columns - 1 : columns] > 0.5
        target = jnp.where(flip_east, rows - 1 - row, row)
        edge = got_ref[shift(base, step + 1), 2 * rows - 3 : 2 * rows - 2, :]
        edge = jnp.sum(jnp.where(lane == target, edge, 0.0), axis=1, keepdims=True)
        end = got_ref[shift(base, step + NTX), 2 * rows - 4 : 2 * rows - 3, :]
        end = jnp.broadcast_to(end, (8, columns))
        end = jnp.where(flip_ends(tile), reversed_lanes(end), end)
        end = jnp.concatenate([end] * (rows // 8), axis=0)
        value = got_ref[tile, 0:rows]
        value = value - jnp.where(lane == columns - 1, edge, 0.0)
        value = value - jnp.where(row == rows - 1, end, 0.0)
        value = jnp.where(wet, value, 0.0)
        out_ref[tile, rows : 2 * rows] = value
        field_ref[pl.ds(first_row(tile), rows), :] = value
        out_ref[tile, 0:rows] = jnp.zeros_like(value)
        return norm + value * value

    def all_of(total):
        return jnp.sum(total, keepdims=True)

    zero = jnp.zeros((rows, columns), jnp.float32)

    def iteration(_, norm):
        def apply(base, step, rolled, total):
            tile = shift(base, step)
            own, east, west, north, south, side, side_turned, ends = neighbours(base, step, rolled)
            others = (
                (east_ref[tile] * east + west_ref[tile] * west)
                + (north_ref[tile] * north + south_ref[tile] * south)
                + (side_ref[tile] * side + turned_ref[tile] * side_turned)
                + ends_ref[tile] * jnp.concatenate([ends] * (rows // 8), axis=0)
            )
            image = total_ref[tile] * own - others
            image_ref[tile] = image
            return total + own * image

        step_size = norm / all_of(over_tiles(apply, zero))

        def advance(base, step, rolled, total):
            tile = shift(base, step)
            out_ref[tile, 0:rows] = out_ref[tile, 0:rows] + step_size * field(tile)
            residual = out_ref[tile, rows : 2 * rows] - step_size * image_ref[tile]
            out_ref[tile, rows : 2 * rows] = residual
            return total + residual * residual

        later = all_of(over_tiles(advance, zero))
        ratio = later / norm

        def turn(base, step, rolled, carry):
            tile = shift(base, step)
            field_ref[pl.ds(first_row(tile), rows), :] = (
                out_ref[tile, rows : 2 * rows] + ratio * field(tile)
            )
            return carry

        over_tiles(turn, 0)
        return later

    lax.fori_loop(0, ITERS, iteration, all_of(over_tiles(begin, zero)))


def cg_of(got, thickness, rows):
    tiles, _, columns = got.shape
    field = pltpu.VMEM((tiles, rows, columns), jnp.float32)
    return pl.pallas_call(
        cg_kernel,
        in_specs=[
            pl.BlockSpec(memory_space=pltpu.SMEM),
            pl.BlockSpec(memory_space=pltpu.VMEM),
        ],
        out_specs=pl.BlockSpec(memory_space=pltpu.VMEM),
        out_shape=jax.ShapeDtypeStruct((tiles, 2 * rows, columns), jnp.float32),
        scratch_shapes=[pltpu.VMEM((tiles * rows + 16, columns), jnp.float32)] + [field] * 9,
        compiler_params=pltpu.CompilerParams(vmem_limit_bytes=LIMIT),
    )(thickness, got)


def on_device(zonal, meridional, fraction, thickness, land_mask, edge_codes):
    tiles = lax.axis_size("tile")
    members, _, rows, columns = zonal.shape
    message = message_of(zonal, meridional, fraction, thickness, land_mask, edge_codes)
    if tiles > members:
        message = jnp.pad(message, ((0, tiles - members), (0, 0), (0, 0)))
    got = lax.all_to_all(message, "tile", split_axis=0, concat_axis=0, tiled=True)
    back = cg_of(got, thickness, rows)
    home = lax.all_to_all(back, "tile", split_axis=0, concat_axis=0, tiled=True)[:members]
    return home[:, :rows], home[:, rows:]


def solution(mesh):
    in_specs = (
        P(None, None, "tile", None),
        P(None, None, "tile", None),
        P(None, "tile", None),
        P(),
        P("tile", None),
        P("tile", None),
    )
    out_specs = (P(None, "tile", None), P(None, "tile", None))
    return jax.shard_map(
        on_device, mesh=mesh, in_specs=in_specs, out_specs=out_specs, check_vma=False
    )
```

time: 90.9 us -> 54.6 us (0.60)
  blocking collectives: 63.3 us -> 41.6 us
  starting transfers between devices: 7.3 us -> 0 us
  other arithmetic: 5.03 us -> 0 us
  local copies, waits for them, and re-layouts: 2.34 us -> 0.82 us
    all_gather x1 -> x0, blocking collectives: 45.1 us -> none  [on_device(): depth = lax.all_gather(depth, 'tile')]
    all_to_all x0 -> x1, blocking collectives: none -> 23 us  [on_device(): lax.all_to_all(message, 'tile', split_axis=0, concat_axis=0, tiled=True)]
    all_to_all x1 -> x0, starting transfers between devices: 7.3 us -> none  [on_device(): lax.all_to_all(message, 'tile', split_axis=0, concat_axis=0, tiled=True)]
    mul x1 -> x0, other arithmetic: 5.03 us -> none  [column_depth(): return wet_cells * running]
  transfers between devices with their start and end apart: 1 -> 0, of which waited for: 0 -> 0; matrix products, arithmetic and copies ran while one was open for 6% -> 0% of each run, Pallas kernels for 0% -> 0%
where the time goes in v1:
time: 54.6 us; the launch traced here: 54.2 us
  blocking collectives  41.6 us (76%)
  Pallas kernels  11.2 us (21%)
  local copies, waits for them, and re-layouts  0.82 us (2%)
  between operations  0.63 us (1%)
    all_to_all x1, blocking collectives, on_device(): lax.all_to_all(message, 'tile', split_axis=0, concat_axis=0, tiled=True)  23 us
    all_to_all x1, blocking collectives, on_device(): lax.all_to_all(back, 'tile', split_axis=0, concat_axis=0, tiled=True)  18.6 us
    pallas_call x1, Pallas kernels, cg_of(): pl.pallas_call(cg_kernel, in_specs=[pl.BlockSpec(memory_space=pltpu.SMEM)...  7.44 us
    pallas_call x1, Pallas kernels, message_of(): pl.pallas_call(message_kernel, grid=(members // step,), in_specs=[pl.Bloc...  3.75 us

profile of v1, /device:TPU:0, one launch (start us, length us, event | category | flops | bytes accessed | tf_op | source)
XLA Modules:
  0.0 54.2 jit_solution(17611977571145726770)
XLA Ops:
  0.6 3.7 %shard_map.77 = f32[32,32,128]{2,1,0:T(8,128)} custom-call(f32[8]{0:T(128)} %thickness_ref.3, s32[1,4]{1,0:T(1,128)} %codes_ref.1, bf16[32,8,16,128]{3,2,1,0:T(8,128)(2,1)} %zonal_ref.1, bf16[32,8,16,128]{3,2,1,0:T(8,128)(2,1)} %meridional_ref.1, bf16[8,16,128]{2,1,0:T(8,128)(2,1)} %fraction_ref.1, s32[16,128]{1,0:T(8,128)} %land_ref.1), custom_call_target="tpu_custom_call" | custom-call | tf_op jit(solution)/shard_map/pallas_call | solution.py:68
  4.4 23.0 %all_to_all.10.got_ref = f32[32,32,128]{2,1,0:T(8,128)} all-to-all(f32[32,32,128]{2,1,0:T(8,128)} %shard_map.77), channel_id=1, replica_groups=mesh['tile'=32] {'tile'}, dimensions={0} | all-to-all | bytes 1048576 | tf_op jit(solution)/shard_map/all_to_all | solution.py:308
  27.3 7.4 %shard_map.78 = f32[32,32,128]{2,1,0:T(8,128)} custom-call(f32[8]{0:T(128)} %thickness_ref.3, f32[32,32,128]{2,1,0:T(8,128)} %all_to_all.10.got_ref), custom_call_target="tpu_custom_call" | custom-call | tf_op jit(solution)/shard_map/pallas_call | solution.py:289
  34.8 18.6 %all_to_all.11 = f32[32,32,128]{2,1,0:T(8,128)S(1)} all-to-all(f32[32,32,128]{2,1,0:T(8,128)} %shard_map.78), channel_id=1, replica_groups=mesh['tile'=32] {'tile'}, dimensions={0} | all-to-all | bytes 1048576 | tf_op jit(solution)/shard_map/all_to_all | solution.py:310
  53.4 0.8 %fusion = (f32[32,16,128]{2,1,0:T(8,128)}, f32[32,16,128]{2,1,0:T(8,128)}) fusion(f32[32,32,128]{2,1,0:T(8,128)S(1)} %all_to_all.11), kind=kLoop, calls=%fused_computation | loop fusion | bytes 1048576 | tf_op jit(solution)/shard_map/slice | solution.py:311

commit v2 on v1

--- a/solution.py
+++ b/solution.py
@@ -10,10 +10,59 @@
 NTX = 16
 ITERS = 4
 CHUNK = 32
-STEPS = 262143.0
-LIMIT = 56 * 1024 * 1024
+STEPS = 1048575.0
+MIDDLE = 4194304.0
 
 coupling_coef = 0.25
+
+
+def power_of_two(exponent):
+    power = lax.shift_left(jnp.ones_like(exponent), exponent & 15).astype(jnp.float32)
+    for bit in (16, 32, 64):
+        power = jnp.where((exponent & bit) != 0, power * 2.0**bit, power)
+    return power
+
+
+def exponent_for(largest):
+    for by in (4, 2, 1):
+        largest = jnp.maximum(largest, pltpu.roll(largest, by, 0))
+    log = jnp.log(jnp.maximum(largest, 2.0**-90)) * 1.4426950408889634
+    return jnp.clip(jnp.floor(log + 0.01).astype(jnp.int32) + 97, 0, 127)
+
+
+def steps_of(values, gain):
+    shifted = jnp.minimum(values * gain + 3.0 * MIDDLE, 4.0 * MIDDLE - 1.0)
+    return shifted.astype(jnp.int32) - int(2.0 * MIDDLE)
+
+
+def packed(upper, lower, exponent, gain):
+    upper = steps_of(upper, gain)
+    lower = steps_of(lower, gain)
+    words = upper | lax.shift_left(lower, 23)
+    high = lax.shift_right_logical(lower, 9)
+    sub = lax.broadcasted_iota(jnp.int32, high.shape, 0)
+    part = lax.shift_right_logical(exponent, 4 * sub) & 15
+    rest = high | lax.shift_left(pltpu.roll(high, 4, 0), 14) | lax.shift_left(part, 28)
+    return words, rest
+
+
+def gain_of(exponent):
+    return power_of_two(127 - exponent) * 2.0**-9
+
+
+def unpacked(words, rest):
+    sub = lax.broadcasted_iota(jnp.int32, words.shape, 0)
+    part = lax.shift_right_logical(rest, 28)
+    exponent = part[0:1] + 16 * part[1:2]
+    step = power_of_two(exponent) * 2.0**-118
+    upper = words & 0x7FFFFF
+    high = jnp.where(sub < 4, rest, pltpu.roll(lax.shift_right_logical(rest, 14), 4, 0)) & 0x3FFF
+    lower = lax.shift_right_logical(words, 23) | lax.shift_left(high, 9)
+    return (
+        (upper.astype(jnp.float32) - MIDDLE) * step,
+        (lower.astype(jnp.float32) - MIDDLE) * step,
+        step,
+    )
 
 
 def message_kernel(
@@ -23,20 +72,26 @@
     lane = lax.broadcasted_iota(jnp.int32, (rows, columns), 1)
     row = lax.broadcasted_iota(jnp.int32, (rows, columns), 0)
     place = lax.broadcasted_iota(jnp.int32, (8, columns), 0)
-    wide = lax.broadcasted_iota(jnp.int32, (8, columns), 1)
-    code = [jnp.where(codes_ref[0, side] == 1, 1.0, 0.0) for side in range(4)]
+    code = [jnp.where(codes_ref[0, side] == 1, 1 << (23 + side), 0) for side in range(4)]
+    flags = (code[0] + code[1]) + (code[2] + code[3])
     parts = [
         thickness_ref[level] * fraction_ref[level].astype(jnp.float32) for level in range(levels)
     ]
     depth = functools.reduce(lambda one, other: one + other, parts)
-    whole = sum_of(thickness_ref, levels)
-    steps = jnp.floor(jnp.where(land_ref[...] == 1, depth * (STEPS / whole), 0.0) + 0.5)
+    scale = STEPS / sum_of(thickness_ref, levels)
+    steps = jnp.where(land_ref[...] == 1, depth * scale + 0.5, 0.0).astype(jnp.int32)
     upper, lower = steps[0:8], steps[8:16]
-    high = jnp.floor(lower * (1.0 / 64.0))
-    words = upper + 262144.0 * (lower - 64.0 * high)
-    rest = high + 4096.0 * pltpu.roll(high, 4, 0)
-    rest = jnp.where(place == 6, jnp.where(wide >= columns // 2, code[0], code[1]), rest)
-    rest = jnp.where(place == 7, code[2] + 2.0 * code[3], rest)
+    pairs = lax.shift_right_logical(upper, 4) | lax.shift_left(
+        lax.shift_right_logical(lower, 4), 16
+    )
+
+    def gathered(values):
+        values = lax.shift_left(values & 15, 4 * place)
+        for by in (4, 2, 1):
+            values = values | pltpu.roll(values, by, 0)
+        return values
+
+    low = jnp.where(place == 6, gathered(upper), gathered(lower))
     for member in range(members):
         along = parts[0] * zonal_ref[member, 0].astype(jnp.float32)
         across = parts[0] * meridional_ref[member, 0].astype(jnp.float32)
@@ -45,13 +100,20 @@
             across = across + parts[level] * meridional_ref[member, level].astype(jnp.float32)
         east = jnp.where(lane == columns - 1, 0.0, pltpu.roll(along, columns - 1, 1))
         north = jnp.where(row == rows - 1, 0.0, pltpu.roll(across, rows - 1, 0))
-        out_ref[member, 0:rows] = along - east + across - north
+        value = along - east + across - north
         first = jnp.where(lane == row, along[:, 0:1], 0.0)
-        first = jnp.sum(first, axis=0, keepdims=True)
-        out_ref[member, rows : rows + 8] = words
-        out_ref[member, rows + 8 : rows + 16] = jnp.where(
-            place == 4, across[0:1], jnp.where(place == 5, first, rest)
-        )
+        first = first[0:8] + first[8:16]
+        for by in (4, 2, 1):
+            first = first + pltpu.roll(first, by, 0)
+        edges = jnp.where(place == 5, first, across[0:1])
+        largest = jnp.maximum(jnp.abs(value[0:8]), jnp.abs(value[8:16]))
+        exponent = exponent_for(jnp.maximum(largest, jnp.abs(edges)))
+        gain = gain_of(exponent)
+        words, rest = packed(value[0:8], value[8:16], exponent, gain)
+        edges = steps_of(edges, gain) | flags
+        out_ref[member, 0:8] = words
+        out_ref[member, 8:16] = jnp.where(place < 4, rest, jnp.where(place < 6, edges, low))
+        out_ref[member, 16:24] = pairs
 
 
 def sum_of(thickness_ref, levels):
@@ -76,9 +138,9 @@
             pl.BlockSpec((levels, rows, columns), lambda at: (0, 0, 0)),
             pl.BlockSpec((rows, columns), lambda at: (0, 0)),
         ],
-        out_specs=pl.BlockSpec((step, 2 * rows, columns), lambda at: (at, 0, 0)),
-        out_shape=jax.ShapeDtypeStruct((members, 2 * rows, columns), jnp.float32),
-        compiler_params=pltpu.CompilerParams(vmem_limit_bytes=LIMIT),
+        out_specs=pl.BlockSpec((step, 24, columns), lambda at: (at, 0, 0)),
+        out_shape=jax.ShapeDtypeStruct((members, 24, columns), jnp.int32),
+        compiler_params=pltpu.CompilerParams(vmem_limit_bytes=8 << 20),
     )(thickness, codes, zonal, meridional, fraction, land_mask)
 
 
@@ -114,6 +176,8 @@
     side_ref,
     turned_ref,
     ends_ref,
+    surface_ref,
+    residual_ref,
 ):
     tiles, rows, columns = image_ref.shape
     levels = thickness_ref.shape[0]
@@ -151,13 +215,15 @@
             rolled[key] = pltpu.roll(field(shift(base, step)), by, 1)
         return rolled[key]
 
+    def flips(tile, one, other, mask):
+        code = jnp.where(mask, 1 << (23 + one), 1 << (23 + other))
+        return (got_ref[tile, 12:13, :] & code) != 0
+
     def flip_sides(tile):
-        return got_ref[tile, 2 * rows - 2 : 2 * rows - 1, :] > 0.5
+        return flips(tile, 0, 1, lane >= columns // 2)
 
     def flip_ends(tile):
-        both = got_ref[tile, 2 * rows - 1 : 2 * rows, :]
-        south = jnp.where(both > 1.5, 1.0, 0.0)
-        return jnp.where(near == 7, both - 2.0 * south, south) > 0.5
+        return flips(tile, 2, 3, near == 7)
 
     def neighbours(base, step, rolled):
         tile = shift(base, step)
@@ -184,15 +250,13 @@
 
     def read_depth(base, step, rolled, carry):
         tile = shift(base, step)
-        words = got_ref[tile, rows : rows + 8, :]
-        rest = got_ref[tile, rows + 8 : rows + 16, :]
-        low = jnp.floor(words * (1.0 / 262144.0))
-        upper = words - 262144.0 * low
-        second = jnp.floor(rest * (1.0 / 4096.0))
-        high = jnp.where(near < 4, rest - 4096.0 * second, pltpu.roll(second, 4, 0))
-        lower = low + 64.0 * high
-        depth = jnp.concatenate([upper, lower], axis=0) * (levels_sum / STEPS)
-        field_ref[pl.ds(first_row(tile), rows), :] = jnp.sqrt(depth)
+        pairs = got_ref[tile, 16:24, :]
+        upper = lax.shift_left(pairs & 0xFFFF, 4)
+        lower = lax.shift_left(lax.shift_right_logical(pairs, 16), 4)
+        upper = upper | lax.shift_right_logical(got_ref[tile, 14:15, :], 4 * near) & 15
+        lower = lower | lax.shift_right_logical(got_ref[tile, 15:16, :], 4 * near) & 15
+        steps = jnp.concatenate([upper, lower], axis=0).astype(jnp.float32)
+        field_ref[pl.ds(first_row(tile), rows), :] = jnp.sqrt(steps * (levels_sum / STEPS))
         return carry
 
     over_tiles(read_depth, 0)
@@ -220,23 +284,32 @@
     over_tiles(weights, 0)
 
     def begin(base, step, rolled, norm):
+        def read(by):
+            key = by % tiles
+            if key not in rolled:
+                other = shift(base, by)
+                rolled[key] = unpacked(got_ref[other, 0:8, :], got_ref[other, 8:16, :])
+            return rolled[key]
+
+        def edge_of(by, at):
+            steps = got_ref[shift(base, by), at : at + 1, :] & 0x7FFFFF
+            return (steps.astype(jnp.float32) - MIDDLE) * read(by)[2]
+
         tile = shift(base, step)
         wet = field(tile) > 0.0
-        flip_east = got_ref[tile, 2 * rows - 2 : 2 * rows - 1, columns - 1 : columns] > 0.5
-        target = jnp.where(flip_east, rows - 1 - row, row)
-        edge = got_ref[shift(base, step + 1), 2 * rows - 3 : 2 * rows - 2, :]
-        edge = jnp.sum(jnp.where(lane == target, edge, 0.0), axis=1, keepdims=True)
-        end = got_ref[shift(base, step + NTX), 2 * rows - 4 : 2 * rows - 3, :]
-        end = jnp.broadcast_to(end, (8, columns))
+        upper, lower, _ = read(step)
+        value = jnp.concatenate([upper, lower], axis=0)
+        target = jnp.where(flip_sides(tile)[:, columns - 1 : columns], rows - 1 - row, row)
+        edge = jnp.where(lane == target, edge_of(step + 1, 13), 0.0)
+        edge = jnp.sum(edge, axis=1, keepdims=True)
+        end = jnp.broadcast_to(edge_of(step + NTX, 12), (8, columns))
         end = jnp.where(flip_ends(tile), reversed_lanes(end), end)
         end = jnp.concatenate([end] * (rows // 8), axis=0)
-        value = got_ref[tile, 0:rows]
         value = value - jnp.where(lane == columns - 1, edge, 0.0)
         value = value - jnp.where(row == rows - 1, end, 0.0)
         value = jnp.where(wet, value, 0.0)
-        out_ref[tile, rows : 2 * rows] = value
-        field_ref[pl.ds(first_row(tile), rows), :] = value
-        out_ref[tile, 0:rows] = jnp.zeros_like(value)
+        residual_ref[tile] = value
+        surface_ref[tile] = jnp.zeros_like(value)
         return norm + value * value
 
     def all_of(total):
@@ -244,7 +317,16 @@
 
     zero = jnp.zeros((rows, columns), jnp.float32)
 
-    def iteration(_, norm):
+    def iteration(_, state):
+        norm, ratio = state
+
+        def turn(base, step, rolled, carry):
+            tile = shift(base, step)
+            field_ref[pl.ds(first_row(tile), rows), :] = residual_ref[tile] + ratio * field(tile)
+            return carry
+
+        over_tiles(turn, 0)
+
         def apply(base, step, rolled, total):
             tile = shift(base, step)
             own, east, west, north, south, side, side_turned, ends = neighbours(base, step, rolled)
@@ -262,25 +344,30 @@
 
         def advance(base, step, rolled, total):
             tile = shift(base, step)
-            out_ref[tile, 0:rows] = out_ref[tile, 0:rows] + step_size * field(tile)
-            residual = out_ref[tile, rows : 2 * rows] - step_size * image_ref[tile]
-            out_ref[tile, rows : 2 * rows] = residual
+            surface_ref[tile] = surface_ref[tile] + step_size * field(tile)
+            residual = residual_ref[tile] - step_size * image_ref[tile]
+            residual_ref[tile] = residual
             return total + residual * residual
 
         later = all_of(over_tiles(advance, zero))
-        ratio = later / norm
-
-        def turn(base, step, rolled, carry):
-            tile = shift(base, step)
-            field_ref[pl.ds(first_row(tile), rows), :] = (
-                out_ref[tile, rows : 2 * rows] + ratio * field(tile)
-            )
-            return carry
-
-        over_tiles(turn, 0)
-        return later
-
-    lax.fori_loop(0, ITERS, iteration, all_of(over_tiles(begin, zero)))
+        return later, later / norm
+
+    norm = all_of(over_tiles(begin, zero))
+    lax.fori_loop(0, ITERS, iteration, (norm, jnp.zeros_like(norm)))
+
+    def finish(base, step, rolled, carry):
+        tile = shift(base, step)
+        rests = []
+        for at, ref in ((0, surface_ref), (16, residual_ref)):
+            upper, lower = ref[tile, 0:8], ref[tile, 8:16]
+            exponent = exponent_for(jnp.maximum(jnp.abs(upper), jnp.abs(lower)))
+            words, rest = packed(upper, lower, exponent, gain_of(exponent))
+            out_ref[tile, at : at + 8] = words
+            rests.append(rest)
+        out_ref[tile, 8:16] = jnp.where(near < 4, rests[0], pltpu.roll(rests[1], 4, 0))
+        return carry
+
+    over_tiles(finish, 0)
 
 
 def cg_of(got, thickness, rows):
@@ -293,10 +380,37 @@
             pl.BlockSpec(memory_space=pltpu.VMEM),
         ],
         out_specs=pl.BlockSpec(memory_space=pltpu.VMEM),
-        out_shape=jax.ShapeDtypeStruct((tiles, 2 * rows, columns), jnp.float32),
-        scratch_shapes=[pltpu.VMEM((tiles * rows + 16, columns), jnp.float32)] + [field] * 9,
-        compiler_params=pltpu.CompilerParams(vmem_limit_bytes=LIMIT),
+        out_shape=jax.ShapeDtypeStruct(got.shape, jnp.int32),
+        scratch_shapes=[pltpu.VMEM((tiles * rows + 16, columns), jnp.float32)] + [field] * 11,
+        compiler_params=pltpu.CompilerParams(
+            vmem_limit_bytes=(4 << 20) + 16 * tiles * rows * columns * 4
+        ),
     )(thickness, got)
+
+
+def home_kernel(home_ref, surface_ref, residual_ref):
+    for member in range(home_ref.shape[0]):
+        rest = home_ref[member, 8:16]
+        upper, lower, _ = unpacked(home_ref[member, 0:8], rest)
+        surface_ref[member, 0:8] = upper
+        surface_ref[member, 8:16] = lower
+        upper, lower, _ = unpacked(home_ref[member, 16:24], pltpu.roll(rest, 4, 0))
+        residual_ref[member, 0:8] = upper
+        residual_ref[member, 8:16] = lower
+
+
+def home_of(home, members, rows):
+    columns = home.shape[2]
+    step = 8 if members % 8 == 0 else 1
+    result = jax.ShapeDtypeStruct((members, rows, columns), jnp.float32)
+    return pl.pallas_call(
+        home_kernel,
+        grid=(members // step,),
+        in_specs=[pl.BlockSpec((step,) + home.shape[1:], lambda at: (at, 0, 0))],
+        out_specs=[pl.BlockSpec((step, rows, columns), lambda at: (at, 0, 0))] * 2,
+        out_shape=[result, result],
+        compiler_params=pltpu.CompilerParams(vmem_limit_bytes=8 << 20),
+    )(home)
 
 
 def on_device(zonal, meridional, fraction, thickness, land_mask, edge_codes):
@@ -307,8 +421,8 @@
         message = jnp.pad(message, ((0, tiles - members), (0, 0), (0, 0)))
     got = lax.all_to_all(message, "tile", split_axis=0, concat_axis=0, tiled=True)
     back = cg_of(got, thickness, rows)
-    home = lax.all_to_all(back, "tile", split_axis=0, concat_axis=0, tiled=True)[:members]
-    return home[:, :rows], home[:, rows:]
+    home = lax.all_to_all(back, "tile", split_axis=0, concat_axis=0, tiled=True)
+    return tuple(home_of(home, members, rows))
 
 
 def solution(mesh):

time: 54.6 us -> 51.3 us (0.940)
  blocking collectives: 41.6 us -> 35.9 us
  local copies, waits for them, and re-layouts: 0.82 us -> 5.21 us
  Pallas kernels: 11.2 us -> 9.22 us
    unnamed x0 -> x12, local copies, waits for them, and re-layouts: none -> 5.21 us
    all_to_all x1, blocking collectives: 18.6 us -> 15.6 us  [on_device(): home = lax.all_to_all(back, 'tile', split_axis=0, concat_axis=0, tiled=True)]
    all_to_all x1, blocking collectives: 23 us -> 20.3 us  [on_device(): lax.all_to_all(message, 'tile', split_axis=0, concat_axis=0, tiled=True)]
    pallas_call x1, Pallas kernels: 3.75 us -> 1.54 us  [message_of(): pl.pallas_call(message_kernel, grid=(members // step,), in_specs=[pl.Bloc...]
    pallas_call x0 -> x1, Pallas kernels: none -> 1.55 us  [home_of(): pl.pallas_call(home_kernel, grid=(members // step,), in_specs=[pl.BlockSp...]
    pallas_call x1, Pallas kernels: 7.44 us -> 6.12 us  [cg_of(): pl.pallas_call(cg_kernel, in_specs=[pl.BlockSpec(memory_space=pltpu.SMEM)...]
    slice x1 -> x0, local copies, waits for them, and re-layouts: 0.82 us -> none  [on_device(): return (home[:, :rows], home[:, rows:])]
where the time goes in v2:
time: 51.3 us; the launch traced here: 51 us
  blocking collectives  35.9 us (70%)
  Pallas kernels  9.22 us (18%)
  local copies, waits for them, and re-layouts  5.21 us (10%)
  between operations  0.65 us (1%)
    all_to_all x1, blocking collectives, on_device(): lax.all_to_all(message, 'tile', split_axis=0, concat_axis=0, tiled=True)  20.3 us
    all_to_all x1, blocking collectives, on_device(): home = lax.all_to_all(back, 'tile', split_axis=0, concat_axis=0, tiled=True)  15.6 us
    pallas_call x1, Pallas kernels, cg_of(): pl.pallas_call(cg_kernel, in_specs=[pl.BlockSpec(memory_space=pltpu.SMEM)...  6.12 us
    unnamed x12, local copies, waits for them, and re-layouts  5.21 us
    pallas_call x1, Pallas kernels, home_of(): pl.pallas_call(home_kernel, grid=(members // step,), in_specs=[pl.BlockSp...  1.55 us
    pallas_call x1, Pallas kernels, message_of(): pl.pallas_call(message_kernel, grid=(members // step,), in_specs=[pl.Bloc...  1.54 us

profile of v2, /device:TPU:0, one launch (start us, length us, event | category | flops | bytes accessed | tf_op | source)
XLA Modules:
  0.0 51.0 jit_solution(10864638149366822819)
XLA Ops:
  0.6 0.0 copy-start
  0.6 1.2 %copy-done = bf16[32,8,16,128]{3,2,1,0:T(8,128)(2,1)S(1)} copy-done((bf16[32,8,16,128]{3,2,1,0:T(8,128)(2,1)S(1)}, bf16[32,8,16,128]{3,2,1,0:T(8,128)(2,1)}, u32[]{:S(2)}) %copy-start) | copy-done | bytes 1048600
  1.9 0.0 copy-start.1
  1.9 1.2 %copy-done.1 = bf16[32,8,16,128]{3,2,1,0:T(8,128)(2,1)S(1)} copy-done((bf16[32,8,16,128]{3,2,1,0:T(8,128)(2,1)S(1)}, bf16[32,8,16,128]{3,2,1,0:T(8,128)(2,1)}, u32[]{:S(2)}) %copy-start.1) | copy-done | bytes 1048600
  3.1 0.0 copy-start.2
  3.1 0.8 %copy-done.2 = bf16[8,16,128]{2,1,0:T(8,128)(2,1)S(1)} copy-done((bf16[8,16,128]{2,1,0:T(8,128)(2,1)S(1)}, bf16[8,16,128]{2,1,0:T(8,128)(2,1)}, u32[]{:S(2)}) %copy-start.2) | copy-done | bytes 32792
  3.8 0.0 copy-start.3
  3.8 0.7 %copy-done.3 = s32[16,128]{1,0:T(8,128)S(1)} copy-done((s32[16,128]{1,0:T(8,128)S(1)}, s32[16,128]{1,0:T(8,128)}, u32[]{:S(2)}) %copy-start.3) | copy-done | bytes 8216
  4.5 0.0 copy-start.4
  4.5 0.7 %copy-done.4 = f32[8]{0:T(128)S(1)} copy-done((f32[8]{0:T(128)S(1)}, f32[8]{0:T(128)}, u32[]{:S(2)}) %copy-start.4) | copy-done | bytes 56
  5.2 0.0 copy-start.5
  5.2 0.7 %copy-done.5 = s32[1,4]{1,0:T(1,128)S(1)} copy-done((s32[1,4]{1,0:T(1,128)S(1)}, s32[1,4]{1,0:T(1,128)}, u32[]{:S(2)}) %copy-start.5) | copy-done | bytes 40
  5.8 1.5 %shard_map.77 = s32[32,24,128]{2,1,0:T(8,128)S(1)} custom-call(f32[8]{0:T(128)S(1)} %copy-done.4, s32[1,4]{1,0:T(1,128)S(1)} %copy-done.5, bf16[32,8,16,128]{3,2,1,0:T(8,128)(2,1)S(1)} %copy-done, bf16[32,8,16,128]{3,2,1,0:T(8,128)(2,1)S(1)} %copy-done.1, bf16[8,16,128]{2,1,0:T(8,128)(2,1)S(1)} %copy-done.2, s32[16,128]{1,0:T(8,128)S(1)} %copy-done.3), custom_call_target="tpu_custom_call" | custom-call | tf_op jit(solution)/shard_map/pallas_call | solution.py:130
  7.4 20.3 %all_to_all.10.got_ref = s32[32,24,128]{2,1,0:T(8,128)S(1)} all-to-all(s32[32,24,128]{2,1,0:T(8,128)S(1)} %shard_map.77), channel_id=1, replica_groups=mesh['tile'=32] {'tile'}, dimensions={0} | all-to-all | bytes 786432 | tf_op jit(solution)/shard_map/all_to_all | solution.py:422
  27.7 6.1 %shard_map.78 = s32[32,24,128]{2,1,0:T(8,128)S(1)} custom-call(f32[8]{0:T(128)S(1)} %copy-done.4, s32[32,24,128]{2,1,0:T(8,128)S(1)} %all_to_all.10.got_ref), custom_call_target="tpu_custom_call" | custom-call | tf_op jit(solution)/shard_map/pallas_call | solution.py:376
  33.8 15.6 %all_to_all.11.home_ref = s32[32,24,128]{2,1,0:T(8,128)S(1)} all-to-all(s32[32,24,128]{2,1,0:T(8,128)S(1)} %shard_map.78), channel_id=1, replica_groups=mesh['tile'=32] {'tile'}, dimensions={0} | all-to-all | bytes 786432 | tf_op jit(solution)/shard_map/all_to_all | solution.py:424
  49.4 1.6 %shard_map.79 = (f32[32,16,128]{2,1,0:T(8,128)}, f32[32,16,128]{2,1,0:T(8,128)}) custom-call(s32[32,24,128]{2,1,0:T(8,128)S(1)} %all_to_all.11.home_ref), custom_call_target="tpu_custom_call" | custom-call | tf_op jit(solution)/shard_map/pallas_call | solution.py:406
Async XLA Ops:
  0.6 1.2 %copy-start = (bf16[32,8,16,128]{3,2,1,0:T(8,128)(2,1)S(1)}, bf16[32,8,16,128]{3,2,1,0:T(8,128)(2,1)}, u32[]{:S(2)}) copy-start(bf16[32,8,16,128]{3,2,1,0:T(8,128)(2,1)} %zonal_ref.1) | copy-start | bytes 3145732
  1.9 1.2 %copy-start.1 = (bf16[32,8,16,128]{3,2,1,0:T(8,128)(2,1)S(1)}, bf16[32,8,16,128]{3,2,1,0:T(8,128)(2,1)}, u32[]{:S(2)}) copy-start(bf16[32,8,16,128]{3,2,1,0:T(8,128)(2,1)} %meridional_ref.1) | copy-start | bytes 3145732
  3.1 0.8 %copy-start.2 = (bf16[8,16,128]{2,1,0:T(8,128)(2,1)S(1)}, bf16[8,16,128]{2,1,0:T(8,128)(2,1)}, u32[]{:S(2)}) copy-start(bf16[8,16,128]{2,1,0:T(8,128)(2,1)} %fraction_ref.1) | copy-start | bytes 98308
  3.8 0.7 %copy-start.3 = (s32[16,128]{1,0:T(8,128)S(1)}, s32[16,128]{1,0:T(8,128)}, u32[]{:S(2)}) copy-start(s32[16,128]{1,0:T(8,128)} %land_ref.1) | copy-start | bytes 24580
  4.5 0.7 %copy-start.4 = (f32[8]{0:T(128)S(1)}, f32[8]{0:T(128)}, u32[]{:S(2)}) copy-start(f32[8]{0:T(128)} %thickness_ref.3) | copy-start | bytes 100
  5.2 0.7 %copy-start.5 = (s32[1,4]{1,0:T(1,128)S(1)}, s32[1,4]{1,0:T(1,128)}, u32[]{:S(2)}) copy-start(s32[1,4]{1,0:T(1,128)} %codes_ref.1) | copy-start | bytes 52

commit v3 on v2

--- a/solution.py
+++ b/solution.py
@@ -9,7 +9,7 @@
 
 NTX = 16
 ITERS = 4
-CHUNK = 32
+CHUNK = 8
 STEPS = 1048575.0
 MIDDLE = 4194304.0
 
@@ -66,9 +66,46 @@
 
 
 def message_kernel(
-    thickness_ref, codes_ref, zonal_ref, meridional_ref, fraction_ref, land_ref, out_ref
+    thickness_ref,
+    codes_ref,
+    zonal_hbm,
+    meridional_hbm,
+    fraction_hbm,
+    land_hbm,
+    out_hbm,
+    zonal_ref,
+    meridional_ref,
+    fraction_ref,
+    land_ref,
+    out_ref,
+    in_sems,
+    out_sems,
 ):
     members, levels, rows, columns = zonal_ref.shape
+    group = members // out_sems.shape[0]
+
+    def copies_in(at):
+        part = pl.ds(at * group, group)
+        return (
+            pltpu.make_async_copy(zonal_hbm.at[part], zonal_ref.at[part], in_sems.at[0, at]),
+            pltpu.make_async_copy(
+                meridional_hbm.at[part], meridional_ref.at[part], in_sems.at[1, at]
+            ),
+        )
+
+    def copy_out(at):
+        part = pl.ds(at * group, group)
+        return pltpu.make_async_copy(out_ref.at[part], out_hbm.at[part], out_sems.at[at])
+
+    land_copy = pltpu.make_async_copy(land_hbm, land_ref, in_sems.at[2, 0])
+    fraction_copy = pltpu.make_async_copy(fraction_hbm, fraction_ref, in_sems.at[2, 1])
+    fraction_copy.start()
+    land_copy.start()
+    for at in range(members // group):
+        for copy in copies_in(at):
+            copy.start()
+    fraction_copy.wait()
+    land_copy.wait()
     lane = lax.broadcasted_iota(jnp.int32, (rows, columns), 1)
     row = lax.broadcasted_iota(jnp.int32, (rows, columns), 0)
     place = lax.broadcasted_iota(jnp.int32, (8, columns), 0)
@@ -92,7 +129,8 @@
         return values
 
     low = jnp.where(place == 6, gathered(upper), gathered(lower))
-    for member in range(members):
+
+    def one(member):
         along = parts[0] * zonal_ref[member, 0].astype(jnp.float32)
         across = parts[0] * meridional_ref[member, 0].astype(jnp.float32)
         for level in range(1, levels):
@@ -115,6 +153,18 @@
         out_ref[member, 8:16] = jnp.where(place < 4, rest, jnp.where(place < 6, edges, low))
         out_ref[member, 16:24] = pairs
 
+    def some(at, carry):
+        for copy in copies_in(at):
+            copy.wait()
+        for member in range(group):
+            one(at * group + member)
+        copy_out(at).start()
+        return carry
+
+    lax.fori_loop(0, members // group, some, 0)
+    for at in range(members // group):
+        copy_out(at).wait()
+
 
 def sum_of(thickness_ref, levels):
     whole = thickness_ref[0]
@@ -124,23 +174,24 @@
 
 
 def message_of(zonal, meridional, fraction, thickness, land_mask, codes):
-    members, levels, rows, columns = zonal.shape
-    step = 8 if members % 8 == 0 else 1
-    field = pl.BlockSpec((step, levels, rows, columns), lambda at: (at, 0, 0, 0))
+    members, _, _, columns = zonal.shape
+    group = 8 if members % 8 == 0 else 1
     return pl.pallas_call(
         message_kernel,
-        grid=(members // step,),
-        in_specs=[
-            pl.BlockSpec(memory_space=pltpu.SMEM),
-            pl.BlockSpec(memory_space=pltpu.SMEM),
-            field,
-            field,
-            pl.BlockSpec((levels, rows, columns), lambda at: (0, 0, 0)),
-            pl.BlockSpec((rows, columns), lambda at: (0, 0)),
+        in_specs=[pl.BlockSpec(memory_space=pltpu.SMEM)] * 2
+        + [pl.BlockSpec(memory_space=pl.ANY)] * 4,
+        out_specs=pl.BlockSpec(memory_space=pl.ANY),
+        out_shape=jax.ShapeDtypeStruct((members, 24, columns), jnp.int32),
+        scratch_shapes=[
+            pltpu.VMEM(zonal.shape, zonal.dtype),
+            pltpu.VMEM(meridional.shape, meridional.dtype),
+            pltpu.VMEM(fraction.shape, fraction.dtype),
+            pltpu.VMEM(land_mask.shape, land_mask.dtype),
+            pltpu.VMEM((members, 24, columns), jnp.int32),
+            pltpu.SemaphoreType.DMA((3, max(2, members // group))),
+            pltpu.SemaphoreType.DMA((members // group,)),
         ],
-        out_specs=pl.BlockSpec((step, 24, columns), lambda at: (at, 0, 0)),
-        out_shape=jax.ShapeDtypeStruct((members, 24, columns), jnp.int32),
-        compiler_params=pltpu.CompilerParams(vmem_limit_bytes=8 << 20),
+        compiler_params=pltpu.CompilerParams(vmem_limit_bytes=60 << 20),
     )(thickness, codes, zonal, meridional, fraction, land_mask)
 
 
@@ -401,7 +452,7 @@
 
 def home_of(home, members, rows):
     columns = home.shape[2]
-    step = 8 if members % 8 == 0 else 1
+    step = 16 if members % 16 == 0 else 1
     result = jax.ShapeDtypeStruct((members, rows, columns), jnp.float32)
     return pl.pallas_call(
         home_kernel,

time: 51.3 us -> 49.5 us (0.965)
  local copies, waits for them, and re-layouts: 5.21 us -> 0.01 us
  Pallas kernels: 9.22 us -> 12.5 us
    unnamed x12 -> x2, local copies, waits for them, and re-layouts: 5.21 us -> 0.01 us
    pallas_call x1, Pallas kernels: 6.12 us -> 8.05 us  [cg_of(): pl.pallas_call(cg_kernel, in_specs=[pl.BlockSpec(memory_space=pltpu.SMEM)...]
    pallas_call x1, Pallas kernels: 1.54 us -> 3.41 us  [message_of(): pl.pallas_call(message_kernel, in_specs=[pl.BlockSpec(memory_space=pltpu....]
    pallas_call x1, Pallas kernels: 1.55 us -> 1.03 us  [home_of(): pl.pallas_call(home_kernel, grid=(members // step,), in_specs=[pl.BlockSp...]
where the time goes in v3:
time: 49.5 us; the launch traced here: 49.3 us
  blocking collectives  36.1 us (73%)
  Pallas kernels  12.5 us (25%)
  between operations  0.65 us (1%)
    all_to_all x1, blocking collectives, on_device(): lax.all_to_all(message, 'tile', split_axis=0, concat_axis=0, tiled=True)  20.5 us
    all_to_all x1, blocking collectives, on_device(): home = lax.all_to_all(back, 'tile', split_axis=0, concat_axis=0, tiled=True)  15.6 us
    pallas_call x1, Pallas kernels, cg_of(): pl.pallas_call(cg_kernel, in_specs=[pl.BlockSpec(memory_space=pltpu.SMEM)...  8.05 us
    pallas_call x1, Pallas kernels, message_of(): pl.pallas_call(message_kernel, in_specs=[pl.BlockSpec(memory_space=pltpu....  3.41 us
    pallas_call x1, Pallas kernels, home_of(): pl.pallas_call(home_kernel, grid=(members // step,), in_specs=[pl.BlockSp...  1.03 us

profile of v3, /device:TPU:0, one launch (start us, length us, event | category | flops | bytes accessed | tf_op | source)
XLA Modules:
  0.0 49.3 jit_solution(6928827275652706743)
XLA Ops:
  0.6 3.4 %shard_map.77 = s32[32,24,128]{2,1,0:T(8,128)} custom-call(f32[8]{0:T(128)} %thickness_ref.3, s32[1,4]{1,0:T(1,128)} %codes_ref.1, bf16[32,8,16,128]{3,2,1,0:T(8,128)(2,1)} %zonal_hbm.1, bf16[32,8,16,128]{3,2,1,0:T(8,128)(2,1)} %meridional_hbm.1, bf16[8,16,128]{2,1,0:T(8,128)(2,1)} %fraction_hbm.1, s32[16,128]{1,0:T(8,128)} %land_hbm.1), custom_call_target="tpu_custom_call" | custom-call | tf_op jit(solution)/shard_map/pallas_call | solution.py:179
  4.0 0.0 copy-start
  4.1 20.5 %all_to_all.10.got_ref = s32[32,24,128]{2,1,0:T(8,128)S(1)} all-to-all(s32[32,24,128]{2,1,0:T(8,128)} %shard_map.77), channel_id=1, replica_groups=mesh['tile'=32] {'tile'}, dimensions={0} | all-to-all | bytes 786432 | tf_op jit(solution)/shard_map/all_to_all | solution.py:473
  24.6 0.0 copy-done
  24.6 8.1 %shard_map.78 = s32[32,24,128]{2,1,0:T(8,128)S(1)} custom-call(f32[8]{0:T(128)S(1)} %copy-done, s32[32,24,128]{2,1,0:T(8,128)S(1)} %all_to_all.10.got_ref), custom_call_target="tpu_custom_call" | custom-call | tf_op jit(solution)/shard_map/pallas_call | solution.py:427
  32.6 15.6 %all_to_all.11.home_ref = s32[32,24,128]{2,1,0:T(8,128)S(1)} all-to-all(s32[32,24,128]{2,1,0:T(8,128)S(1)} %shard_map.78), channel_id=1, replica_groups=mesh['tile'=32] {'tile'}, dimensions={0} | all-to-all | bytes 786432 | tf_op jit(solution)/shard_map/all_to_all | solution.py:475
  48.2 1.0 %shard_map.79 = (f32[32,16,128]{2,1,0:T(8,128)}, f32[32,16,128]{2,1,0:T(8,128)}) custom-call(s32[32,24,128]{2,1,0:T(8,128)S(1)} %all_to_all.11.home_ref), custom_call_target="tpu_custom_call" | custom-call | tf_op jit(solution)/shard_map/pallas_call | solution.py:457
Async XLA Ops:
  4.0 20.5 %copy-start = (f32[8]{0:T(128)S(1)}, f32[8]{0:T(128)}, u32[]{:S(2)}) copy-start(f32[8]{0:T(128)} %thickness_ref.3) | copy-start | bytes 100

commit v4 on v3

--- a/solution.py
+++ b/solution.py
@@ -9,9 +9,12 @@
 
 NTX = 16
 ITERS = 4
-CHUNK = 8
-STEPS = 1048575.0
-MIDDLE = 4194304.0
+CHUNK = 32
+BITS = 18
+STEPS = 2.0**BITS - 1.0
+MIDDLE = 2.0 ** (BITS - 1)
+ROUNDING = 2.0**23
+PIECES = 5
 
 coupling_coef = 0.25
 
@@ -31,38 +34,49 @@
 
 
 def steps_of(values, gain):
-    shifted = jnp.minimum(values * gain + 3.0 * MIDDLE, 4.0 * MIDDLE - 1.0)
-    return shifted.astype(jnp.int32) - int(2.0 * MIDDLE)
-
-
-def packed(upper, lower, exponent, gain):
-    upper = steps_of(upper, gain)
-    lower = steps_of(lower, gain)
-    words = upper | lax.shift_left(lower, 23)
-    high = lax.shift_right_logical(lower, 9)
-    sub = lax.broadcasted_iota(jnp.int32, high.shape, 0)
-    part = lax.shift_right_logical(exponent, 4 * sub) & 15
-    rest = high | lax.shift_left(pltpu.roll(high, 4, 0), 14) | lax.shift_left(part, 28)
-    return words, rest
+    shifted = values * gain + (ROUNDING + MIDDLE)
+    return jnp.minimum(shifted, ROUNDING + STEPS).astype(jnp.int32) - int(ROUNDING)
 
 
 def gain_of(exponent):
-    return power_of_two(127 - exponent) * 2.0**-9
-
-
-def unpacked(words, rest):
+    return power_of_two(127 - exponent) * 2.0 ** (96 - 127 + BITS - 1)
+
+
+def gathered(values):
+    sub = lax.broadcasted_iota(jnp.int32, values.shape, 0)
+    values = lax.shift_left(values & 15, 4 * sub)
+    for by in (4, 2, 1):
+        values = values | pltpu.roll(values, by, 0)
+    return values
+
+
+def packed(upper, lower):
+    words = upper | lax.shift_left(lower, BITS)
+    return words, gathered(lax.shift_right_logical(lower, BITS - 4))
+
+
+def unpacked(words, high):
     sub = lax.broadcasted_iota(jnp.int32, words.shape, 0)
-    part = lax.shift_right_logical(rest, 28)
-    exponent = part[0:1] + 16 * part[1:2]
-    step = power_of_two(exponent) * 2.0**-118
-    upper = words & 0x7FFFFF
-    high = jnp.where(sub < 4, rest, pltpu.roll(lax.shift_right_logical(rest, 14), 4, 0)) & 0x3FFF
-    lower = lax.shift_right_logical(words, 23) | lax.shift_left(high, 9)
-    return (
-        (upper.astype(jnp.float32) - MIDDLE) * step,
-        (lower.astype(jnp.float32) - MIDDLE) * step,
-        step,
-    )
+    upper = words & ((1 << BITS) - 1)
+    high = lax.shift_right_logical(jnp.broadcast_to(high, words.shape), 4 * sub) & 15
+    return upper, lax.shift_right_logical(words, BITS) | lax.shift_left(high, BITS - 4)
+
+
+def step_of(exponent):
+    return power_of_two(exponent) * 2.0 ** (-96 - (BITS - 1))
+
+
+def values_of(steps, step):
+    return (steps.astype(jnp.float32) - MIDDLE) * step
+
+
+def eight(ref, at, piece):
+    return jnp.concatenate([ref[at, piece], ref[at, piece + 1]], axis=0)
+
+
+def put_eight(ref, at, piece, values):
+    ref[at, piece] = values[0:4]
+    ref[at, piece + 1] = values[4:8]
 
 
 def message_kernel(
@@ -109,26 +123,16 @@
     lane = lax.broadcasted_iota(jnp.int32, (rows, columns), 1)
     row = lax.broadcasted_iota(jnp.int32, (rows, columns), 0)
     place = lax.broadcasted_iota(jnp.int32, (8, columns), 0)
-    code = [jnp.where(codes_ref[0, side] == 1, 1 << (23 + side), 0) for side in range(4)]
+    code = [jnp.where(codes_ref[0, side] == 1, 1 << (BITS + side), 0) for side in range(4)]
     flags = (code[0] + code[1]) + (code[2] + code[3])
     parts = [
         thickness_ref[level] * fraction_ref[level].astype(jnp.float32) for level in range(levels)
     ]
     depth = functools.reduce(lambda one, other: one + other, parts)
-    scale = STEPS / sum_of(thickness_ref, levels)
-    steps = jnp.where(land_ref[...] == 1, depth * scale + 0.5, 0.0).astype(jnp.int32)
-    upper, lower = steps[0:8], steps[8:16]
-    pairs = lax.shift_right_logical(upper, 4) | lax.shift_left(
-        lax.shift_right_logical(lower, 4), 16
-    )
-
-    def gathered(values):
-        values = lax.shift_left(values & 15, 4 * place)
-        for by in (4, 2, 1):
-            values = values | pltpu.roll(values, by, 0)
-        return values
-
-    low = jnp.where(place == 6, gathered(upper), gathered(lower))
+    root = jnp.sqrt(depth * (1.0 / sum_of(thickness_ref, levels)))
+    steps = jnp.where(land_ref[...] == 1, jnp.minimum(root * STEPS + 0.5, STEPS), 0.0)
+    steps = steps.astype(jnp.int32)
+    roots, roots_high = packed(steps[0:8], steps[8:16])
 
     def one(member):
         along = parts[0] * zonal_ref[member, 0].astype(jnp.float32)
@@ -143,15 +147,18 @@
         first = first[0:8] + first[8:16]
         for by in (4, 2, 1):
             first = first + pltpu.roll(first, by, 0)
-        edges = jnp.where(place == 5, first, across[0:1])
+        edges = jnp.where(place == 3, first, across[0:1])
         largest = jnp.maximum(jnp.abs(value[0:8]), jnp.abs(value[8:16]))
         exponent = exponent_for(jnp.maximum(largest, jnp.abs(edges)))
         gain = gain_of(exponent)
-        words, rest = packed(value[0:8], value[8:16], exponent, gain)
-        edges = steps_of(edges, gain) | flags
-        out_ref[member, 0:8] = words
-        out_ref[member, 8:16] = jnp.where(place < 4, rest, jnp.where(place < 6, edges, low))
-        out_ref[member, 16:24] = pairs
+        words, high = packed(steps_of(value[0:8], gain), steps_of(value[8:16], gain))
+        edges = steps_of(edges, gain) | jnp.where(
+            place == 3, lax.shift_left(exponent, BITS), flags
+        )
+        last = jnp.where(place == 0, high, jnp.where(place == 1, roots_high, edges))
+        put_eight(out_ref, member, 0, words)
+        put_eight(out_ref, member, 2, roots)
+        out_ref[member, 4] = last[0:4]
 
     def some(at, carry):
         for copy in copies_in(at):
@@ -181,13 +188,13 @@
         in_specs=[pl.BlockSpec(memory_space=pltpu.SMEM)] * 2
         + [pl.BlockSpec(memory_space=pl.ANY)] * 4,
         out_specs=pl.BlockSpec(memory_space=pl.ANY),
-        out_shape=jax.ShapeDtypeStruct((members, 24, columns), jnp.int32),
+        out_shape=jax.ShapeDtypeStruct((members, PIECES, 4, columns), jnp.int32),
         scratch_shapes=[
             pltpu.VMEM(zonal.shape, zonal.dtype),
             pltpu.VMEM(meridional.shape, meridional.dtype),
             pltpu.VMEM(fraction.shape, fraction.dtype),
             pltpu.VMEM(land_mask.shape, land_mask.dtype),
-            pltpu.VMEM((members, 24, columns), jnp.int32),
+            pltpu.VMEM((members, PIECES, 4, columns), jnp.int32),
             pltpu.SemaphoreType.DMA((3, max(2, members // group))),
             pltpu.SemaphoreType.DMA((members // group,)),
         ],
@@ -224,6 +231,8 @@
     north_ref,
     south_ref,
     total_ref,
+    direction_ref,
+    product_ref,
     side_ref,
     turned_ref,
     ends_ref,
@@ -267,8 +276,8 @@
         return rolled[key]
 
     def flips(tile, one, other, mask):
-        code = jnp.where(mask, 1 << (23 + one), 1 << (23 + other))
-        return (got_ref[tile, 12:13, :] & code) != 0
+        code = jnp.where(mask, 1 << (BITS + one), 1 << (BITS + other))
+        return (got_ref[tile, 4, 2:3, :] & code) != 0
 
     def flip_sides(tile):
         return flips(tile, 0, 1, lane >= columns // 2)
@@ -301,13 +310,9 @@
 
     def read_depth(base, step, rolled, carry):
         tile = shift(base, step)
-        pairs = got_ref[tile, 16:24, :]
-        upper = lax.shift_left(pairs & 0xFFFF, 4)
-        lower = lax.shift_left(lax.shift_right_logical(pairs, 16), 4)
-        upper = upper | lax.shift_right_logical(got_ref[tile, 14:15, :], 4 * near) & 15
-        lower = lower | lax.shift_right_logical(got_ref[tile, 15:16, :], 4 * near) & 15
+        upper, lower = unpacked(eight(got_ref, tile, 2), got_ref[tile, 4, 1:2, :])
         steps = jnp.concatenate([upper, lower], axis=0).astype(jnp.float32)
-        field_ref[pl.ds(first_row(tile), rows), :] = jnp.sqrt(steps * (levels_sum / STEPS))
+        field_ref[pl.ds(first_row(tile), rows), :] = steps * (1.0 / STEPS)
         return carry
 
     over_tiles(read_depth, 0)
@@ -315,7 +320,7 @@
     def weights(base, step, rolled, carry):
         tile = shift(base, step)
         own, east, west, north, south, side, side_turned, ends = neighbours(base, step, rolled)
-        own = coupling_coef * own
+        own = (coupling_coef * levels_sum) * own
         east = jnp.where(lane == columns - 1, 0.0, own * east)
         west = jnp.where(lane == 0, 0.0, own * west)
         north = jnp.where(row == rows - 1, 0.0, own * north)
@@ -334,95 +339,128 @@
 
     over_tiles(weights, 0)
 
-    def begin(base, step, rolled, norm):
-        def read(by):
+    def begin(base, step, rolled, carry):
+        def step_at(by):
             key = by % tiles
             if key not in rolled:
-                other = shift(base, by)
-                rolled[key] = unpacked(got_ref[other, 0:8, :], got_ref[other, 8:16, :])
+                row_of = got_ref[shift(base, by), 4, 3:4, :]
+                rolled[key] = step_of(lax.shift_right_logical(row_of, BITS))
             return rolled[key]
 
         def edge_of(by, at):
-            steps = got_ref[shift(base, by), at : at + 1, :] & 0x7FFFFF
-            return (steps.astype(jnp.float32) - MIDDLE) * read(by)[2]
+            steps = got_ref[shift(base, by), 4, at : at + 1, :] & ((1 << BITS) - 1)
+            return values_of(steps, step_at(by))
 
         tile = shift(base, step)
         wet = field(tile) > 0.0
-        upper, lower, _ = read(step)
-        value = jnp.concatenate([upper, lower], axis=0)
+        upper, lower = unpacked(eight(got_ref, tile, 0), got_ref[tile, 4, 0:1, :])
+        value = values_of(jnp.concatenate([upper, lower], axis=0), step_at(step))
         target = jnp.where(flip_sides(tile)[:, columns - 1 : columns], rows - 1 - row, row)
-        edge = jnp.where(lane == target, edge_of(step + 1, 13), 0.0)
+        edge = jnp.where(lane == target, edge_of(step + 1, 3), 0.0)
         edge = jnp.sum(edge, axis=1, keepdims=True)
-        end = jnp.broadcast_to(edge_of(step + NTX, 12), (8, columns))
+        end = jnp.broadcast_to(edge_of(step + NTX, 2), (8, columns))
         end = jnp.where(flip_ends(tile), reversed_lanes(end), end)
         end = jnp.concatenate([end] * (rows // 8), axis=0)
         value = value - jnp.where(lane == columns - 1, edge, 0.0)
         value = value - jnp.where(row == rows - 1, end, 0.0)
         value = jnp.where(wet, value, 0.0)
         residual_ref[tile] = value
-        surface_ref[tile] = jnp.zeros_like(value)
-        return norm + value * value
+        return carry
 
     def all_of(total):
         return jnp.sum(total, keepdims=True)
 
     zero = jnp.zeros((rows, columns), jnp.float32)
 
-    def iteration(_, state):
-        norm, ratio = state
-
-        def turn(base, step, rolled, carry):
+    def apply(base, step, rolled, totals):
+        tile = shift(base, step)
+        own, east, west, north, south, side, side_turned, ends = neighbours(base, step, rolled)
+        others = (
+            (east_ref[tile] * east + west_ref[tile] * west)
+            + (north_ref[tile] * north + south_ref[tile] * south)
+            + (side_ref[tile] * side + turned_ref[tile] * side_turned)
+            + ends_ref[tile] * jnp.concatenate([ends] * (rows // 8), axis=0)
+        )
+        image = total_ref[tile] * own - others
+        image_ref[tile] = image
+        return totals[0] + own * own, totals[1] + own * image
+
+    def sums():
+        squares, products = over_tiles(apply, (zero, zero))
+        return all_of(squares), all_of(products)
+
+    def copy_back(base, step, rolled, carry):
+        tile = shift(base, step)
+        field_ref[pl.ds(first_row(tile), rows), :] = residual_ref[tile]
+        return carry
+
+    over_tiles(begin, 0)
+    over_tiles(copy_back, 0)
+
+    norm, product = sums()
+    size = norm / product
+
+    def first(base, step, rolled, carry):
+        tile = shift(base, step)
+        own, image = field(tile), image_ref[tile]
+        direction_ref[tile] = own
+        product_ref[tile] = image
+        surface_ref[tile] = size * own
+        field_ref[pl.ds(first_row(tile), rows), :] = own - size * image
+        return carry
+
+    over_tiles(first, 0)
+
+    def next_sizes(state):
+        norm, size = state
+        later, product = sums()
+        ratio = later / norm
+        return later, ratio, later / (product - ratio * (later / size))
+
+    def middle(_, state):
+        later, ratio, size = next_sizes(state)
+
+        def advance(base, step, rolled, carry):
             tile = shift(base, step)
-            field_ref[pl.ds(first_row(tile), rows), :] = residual_ref[tile] + ratio * field(tile)
+            own = field(tile)
+            direction = own + ratio * direction_ref[tile]
+            image = image_ref[tile] + ratio * product_ref[tile]
+            direction_ref[tile] = direction
+            product_ref[tile] = image
+            surface_ref[tile] = surface_ref[tile] + size * direction
+            field_ref[pl.ds(first_row(tile), rows), :] = own - size * image
             return carry
 
-        over_tiles(turn, 0)
-
-        def apply(base, step, rolled, total):
-            tile = shift(base, step)
-            own, east, west, north, south, side, side_turned, ends = neighbours(base, step, rolled)
-            others = (
-                (east_ref[tile] * east + west_ref[tile] * west)
-                + (north_ref[tile] * north + south_ref[tile] * south)
-                + (side_ref[tile] * side + turned_ref[tile] * side_turned)
-                + ends_ref[tile] * jnp.concatenate([ends] * (rows // 8), axis=0)
-            )
-            image = total_ref[tile] * own - others
-            image_ref[tile] = image
-            return total + own * image
-
-        step_size = norm / all_of(over_tiles(apply, zero))
-
-        def advance(base, step, rolled, total):
-            tile = shift(base, step)
-            surface_ref[tile] = surface_ref[tile] + step_size * field(tile)
-            residual = residual_ref[tile] - step_size * image_ref[tile]
-            residual_ref[tile] = residual
-            return total + residual * residual
-
-        later = all_of(over_tiles(advance, zero))
-        return later, later / norm
-
-    norm = all_of(over_tiles(begin, zero))
-    lax.fori_loop(0, ITERS, iteration, (norm, jnp.zeros_like(norm)))
+        over_tiles(advance, 0)
+        return later, size
+
+    state = lax.fori_loop(1, ITERS - 1, middle, (norm, size))
+    _, ratio, last_size = next_sizes(state)
 
     def finish(base, step, rolled, carry):
         tile = shift(base, step)
-        rests = []
-        for at, ref in ((0, surface_ref), (16, residual_ref)):
-            upper, lower = ref[tile, 0:8], ref[tile, 8:16]
+        own = field(tile)
+        direction = own + ratio * direction_ref[tile]
+        image = image_ref[tile] + ratio * product_ref[tile]
+        results = (surface_ref[tile] + last_size * direction, own - last_size * image)
+        lasts = []
+        for at, result in enumerate(results):
+            upper, lower = result[0:8], result[8:16]
             exponent = exponent_for(jnp.maximum(jnp.abs(upper), jnp.abs(lower)))
-            words, rest = packed(upper, lower, exponent, gain_of(exponent))
-            out_ref[tile, at : at + 8] = words
-            rests.append(rest)
-        out_ref[tile, 8:16] = jnp.where(near < 4, rests[0], pltpu.roll(rests[1], 4, 0))
+            gain = gain_of(exponent)
+            words, high = packed(steps_of(upper, gain), steps_of(lower, gain))
+            put_eight(out_ref, tile, 2 * at, words)
+            lasts += [high, exponent]
+        last = jnp.where(near < 2, jnp.where(near == 0, lasts[0], lasts[1]),
+                         jnp.where(near == 2, lasts[2], lasts[3]))
+        out_ref[tile, 4] = last[0:4]
         return carry
 
     over_tiles(finish, 0)
 
 
 def cg_of(got, thickness, rows):
-    tiles, _, columns = got.shape
+    tiles, columns = got.shape[0], got.shape[-1]
     field = pltpu.VMEM((tiles, rows, columns), jnp.float32)
     return pl.pallas_call(
         cg_kernel,
@@ -432,32 +470,32 @@
         ],
         out_specs=pl.BlockSpec(memory_space=pltpu.VMEM),
         out_shape=jax.ShapeDtypeStruct(got.shape, jnp.int32),
-        scratch_shapes=[pltpu.VMEM((tiles * rows + 16, columns), jnp.float32)] + [field] * 11,
+        scratch_shapes=[pltpu.VMEM((tiles * rows + 16, columns), jnp.float32)] + [field] * 13,
         compiler_params=pltpu.CompilerParams(
-            vmem_limit_bytes=(4 << 20) + 16 * tiles * rows * columns * 4
+            vmem_limit_bytes=(4 << 20) + 18 * tiles * rows * columns * 4
         ),
     )(thickness, got)
 
 
 def home_kernel(home_ref, surface_ref, residual_ref):
     for member in range(home_ref.shape[0]):
-        rest = home_ref[member, 8:16]
-        upper, lower, _ = unpacked(home_ref[member, 0:8], rest)
-        surface_ref[member, 0:8] = upper
-        surface_ref[member, 8:16] = lower
-        upper, lower, _ = unpacked(home_ref[member, 16:24], pltpu.roll(rest, 4, 0))
-        residual_ref[member, 0:8] = upper
-        residual_ref[member, 8:16] = lower
+        for at, ref in enumerate((surface_ref, residual_ref)):
+            upper, lower = unpacked(
+                eight(home_ref, member, 2 * at), home_ref[member, 4, 2 * at : 2 * at + 1, :]
+            )
+            step = step_of(home_ref[member, 4, 2 * at + 1 : 2 * at + 2, :])
+            ref[member, 0:8] = values_of(upper, step)
+            ref[member, 8:16] = values_of(lower, step)
 
 
 def home_of(home, members, rows):
-    columns = home.shape[2]
+    columns = home.shape[-1]
     step = 16 if members % 16 == 0 else 1
     result = jax.ShapeDtypeStruct((members, rows, columns), jnp.float32)
     return pl.pallas_call(
         home_kernel,
         grid=(members // step,),
-        in_specs=[pl.BlockSpec((step,) + home.shape[1:], lambda at: (at, 0, 0))],
+        in_specs=[pl.BlockSpec((step,) + home.shape[1:], lambda at: (at, 0, 0, 0))],
         out_specs=[pl.BlockSpec((step, rows, columns), lambda at: (at, 0, 0))] * 2,
         out_shape=[result, result],
         compiler_params=pltpu.CompilerParams(vmem_limit_bytes=8 << 20),
@@ -469,7 +507,7 @@
     members, _, rows, columns = zonal.shape
     message = message_of(zonal, meridional, fraction, thickness, land_mask, edge_codes)
     if tiles > members:
-        message = jnp.pad(message, ((0, tiles - members), (0, 0), (0, 0)))
+        message = jnp.pad(message, ((0, tiles - members), (0, 0), (0, 0), (0, 0)))
     got = lax.all_to_all(message, "tile", split_axis=0, concat_axis=0, tiled=True)
     back = cg_of(got, thickness, rows)
     home = lax.all_to_all(back, "tile", split_axis=0, concat_axis=0, tiled=True)

time: 49.5 us -> 44.6 us (0.901)
  blocking collectives: 36.1 us -> 33.5 us
  Pallas kernels: 12.5 us -> 10.2 us
    pallas_call x1, Pallas kernels: 8.05 us -> 5.8 us  [cg_of(): pl.pallas_call(cg_kernel, in_specs=[pl.BlockSpec(memory_space=pltpu.SMEM)...]
    all_to_all x1, blocking collectives: 15.6 us -> 14.2 us  [on_device(): home = lax.all_to_all(back, 'tile', split_axis=0, concat_axis=0, tiled=True)]
    all_to_all x1, blocking collectives: 20.5 us -> 19.3 us  [on_device(): lax.all_to_all(message, 'tile', split_axis=0, concat_axis=0, tiled=True)]
where the time goes in v4:
time: 44.6 us; the launch traced here: 44.4 us
  blocking collectives  33.5 us (75%)
  Pallas kernels  10.2 us (23%)
  between operations  0.65 us (1%)
    all_to_all x1, blocking collectives, on_device(): lax.all_to_all(message, 'tile', split_axis=0, concat_axis=0, tiled=True)  19.3 us
    all_to_all x1, blocking collectives, on_device(): home = lax.all_to_all(back, 'tile', split_axis=0, concat_axis=0, tiled=True)  14.2 us
    pallas_call x1, Pallas kernels, cg_of(): pl.pallas_call(cg_kernel, in_specs=[pl.BlockSpec(memory_space=pltpu.SMEM)...  5.8 us
    pallas_call x1, Pallas kernels, message_of(): pl.pallas_call(message_kernel, in_specs=[pl.BlockSpec(memory_space=pltpu....  3.41 us
    pallas_call x1, Pallas kernels, home_of(): pl.pallas_call(home_kernel, grid=(members // step,), in_specs=[pl.BlockSp...  0.99 us

profile of v4, /device:TPU:0, one launch (start us, length us, event | category | flops | bytes accessed | tf_op | source)
XLA Modules:
  0.0 44.4 jit_solution(16681886160563934276)
XLA Ops:
  0.6 3.4 %shard_map.77 = s32[32,5,4,128]{3,2,1,0:T(4,128)} custom-call(f32[8]{0:T(128)} %thickness_ref.3, s32[1,4]{1,0:T(1,128)} %codes_ref.1, bf16[32,8,16,128]{3,2,1,0:T(8,128)(2,1)} %zonal_hbm.1, bf16[32,8,16,128]{3,2,1,0:T(8,128)(2,1)} %meridional_hbm.1, bf16[8,16,128]{2,1,0:T(8,128)(2,1)} %fraction_hbm.1, s32[16,128]{1,0:T(8,128)} %land_hbm.1), custom_call_target="tpu_custom_call" | custom-call | tf_op jit(solution)/shard_map/pallas_call | solution.py:186
  4.1 0.0 copy-start
  4.1 19.3 %all_to_all.10.got_ref = s32[32,5,4,128]{3,2,1,0:T(4,128)S(1)} all-to-all(s32[32,5,4,128]{3,2,1,0:T(4,128)} %shard_map.77), channel_id=1, replica_groups=mesh['tile'=32] {'tile'}, dimensions={0} | all-to-all | bytes 655360 | tf_op jit(solution)/shard_map/all_to_all | solution.py:511
  23.4 0.0 copy-done
  23.4 5.8 %shard_map.78 = s32[32,5,4,128]{3,2,1,0:T(4,128)S(1)} custom-call(f32[8]{0:T(128)S(1)} %copy-done, s32[32,5,4,128]{3,2,1,0:T(4,128)S(1)} %all_to_all.10.got_ref), custom_call_target="tpu_custom_call" | custom-call | tf_op jit(solution)/shard_map/pallas_call | solution.py:465
  29.2 14.2 %all_to_all.11.home_ref = s32[32,5,4,128]{3,2,1,0:T(4,128)S(1)} all-to-all(s32[32,5,4,128]{3,2,1,0:T(4,128)S(1)} %shard_map.78), channel_id=1, replica_groups=mesh['tile'=32] {'tile'}, dimensions={0} | all-to-all | bytes 655360 | tf_op jit(solution)/shard_map/all_to_all | solution.py:513
  43.4 1.0 %shard_map.79 = (f32[32,16,128]{2,1,0:T(8,128)}, f32[32,16,128]{2,1,0:T(8,128)}) custom-call(s32[32,5,4,128]{3,2,1,0:T(4,128)S(1)} %all_to_all.11.home_ref), custom_call_target="tpu_custom_call" | custom-call | tf_op jit(solution)/shard_map/pallas_call | solution.py:495
Async XLA Ops:
  4.1 19.3 %copy-start = (f32[8]{0:T(128)S(1)}, f32[8]{0:T(128)}, u32[]{:S(2)}) copy-start(f32[8]{0:T(128)} %thickness_ref.3) | copy-start | bytes 100

commit v5 on v4

--- a/solution.py
+++ b/solution.py
@@ -182,7 +182,7 @@
 
 def message_of(zonal, meridional, fraction, thickness, land_mask, codes):
     members, _, _, columns = zonal.shape
-    group = 8 if members % 8 == 0 else 1
+    group = 4 if members % 4 == 0 else 1
     return pl.pallas_call(
         message_kernel,
         in_specs=[pl.BlockSpec(memory_space=pltpu.SMEM)] * 2
@@ -237,7 +237,7 @@
     turned_ref,
     ends_ref,
     surface_ref,
-    residual_ref,
+    root_ref,
 ):
     tiles, rows, columns = image_ref.shape
     levels = thickness_ref.shape[0]
@@ -266,13 +266,13 @@
         at = tile * rows + 8
         return at if isinstance(at, int) else pl.multiple_of(at, 8)
 
-    def field(tile, by=0):
-        return field_ref[pl.ds(first_row(tile) + by, rows), :]
-
-    def turned(base, step, rolled, by):
+    def field(tile, by=0, ref=field_ref):
+        return ref[pl.ds(first_row(tile) + by, rows), :]
+
+    def turned(base, step, rolled, by, ref):
         key = (step, by)
         if key not in rolled:
-            rolled[key] = pltpu.roll(field(shift(base, step)), by, 1)
+            rolled[key] = pltpu.roll(field(shift(base, step), 0, ref), by, 1)
         return rolled[key]
 
     def flips(tile, one, other, mask):
@@ -285,41 +285,46 @@
     def flip_ends(tile):
         return flips(tile, 2, 3, near == 7)
 
-    def neighbours(base, step, rolled):
+    def neighbours(base, step, rolled, ref):
         tile = shift(base, step)
-        own = field(tile)
-        east = turned(base, step, rolled, columns - 1)
-        west = turned(base, step, rolled, 1)
+        own = field(tile, 0, ref)
+        east = turned(base, step, rolled, columns - 1, ref)
+        west = turned(base, step, rolled, 1, ref)
         side = jnp.where(
             lane >= columns // 2,
-            turned(base, step + 1, rolled, columns - 1),
-            turned(base, step - 1, rolled, 1),
+            turned(base, step + 1, rolled, columns - 1, ref),
+            turned(base, step - 1, rolled, 1, ref),
         )
         ends = jnp.where(
             near == 7,
-            field_ref[pl.ds(first_row(shift(base, step + NTX)), 1), :],
-            field_ref[pl.ds(first_row(shift(base, step - NTX)) + rows - 1, 1), :],
+            ref[pl.ds(first_row(shift(base, step + NTX)), 1), :],
+            ref[pl.ds(first_row(shift(base, step - NTX)) + rows - 1, 1), :],
         )
         ends = jnp.where(flip_ends(tile), reversed_lanes(ends), ends)
-        return own, east, west, field(tile, 1), field(tile, -1), side, reversed_rows(side), ends
+        north, south = field(tile, 1, ref), field(tile, -1, ref)
+        return own, east, west, north, south, side, reversed_rows(side), ends
 
     levels_sum = sum_of(thickness_ref, levels)
     padding = jnp.zeros((8, columns), jnp.float32)
-    field_ref[0:8, :] = padding
-    field_ref[tiles * rows + 8 : tiles * rows + 16, :] = padding
+    for ref in (field_ref, root_ref):
+        ref[0:8, :] = padding
+        ref[tiles * rows + 8 : tiles * rows + 16, :] = padding
 
     def read_depth(base, step, rolled, carry):
         tile = shift(base, step)
         upper, lower = unpacked(eight(got_ref, tile, 2), got_ref[tile, 4, 1:2, :])
         steps = jnp.concatenate([upper, lower], axis=0).astype(jnp.float32)
-        field_ref[pl.ds(first_row(tile), rows), :] = steps * (1.0 / STEPS)
+        root_ref[pl.ds(first_row(tile), rows), :] = steps * (1.0 / STEPS)
         return carry
 
     over_tiles(read_depth, 0)
 
     def weights(base, step, rolled, carry):
         tile = shift(base, step)
-        own, east, west, north, south, side, side_turned, ends = neighbours(base, step, rolled)
+        own, east, west, north, south, side, side_turned, ends = neighbours(
+            base, step, rolled, root_ref
+        )
+        wet = own > 0.0
         own = (coupling_coef * levels_sum) * own
         east = jnp.where(lane == columns - 1, 0.0, own * east)
         west = jnp.where(lane == 0, 0.0, own * west)
@@ -335,13 +340,9 @@
         both = jnp.concatenate([upper, lower], axis=0)
         ends_ref[tile] = both
         total_ref[tile] = 1.0 + ((east + west) + (north + south)) + (side + both)
-        return carry
-
-    over_tiles(weights, 0)
-
-    def begin(base, step, rolled, carry):
+
         def step_at(by):
-            key = by % tiles
+            key = ("step", by % tiles)
             if key not in rolled:
                 row_of = got_ref[shift(base, by), 4, 3:4, :]
                 rolled[key] = step_of(lax.shift_right_logical(row_of, BITS))
@@ -351,8 +352,6 @@
             steps = got_ref[shift(base, by), 4, at : at + 1, :] & ((1 << BITS) - 1)
             return values_of(steps, step_at(by))
 
-        tile = shift(base, step)
-        wet = field(tile) > 0.0
         upper, lower = unpacked(eight(got_ref, tile, 0), got_ref[tile, 4, 0:1, :])
         value = values_of(jnp.concatenate([upper, lower], axis=0), step_at(step))
         target = jnp.where(flip_sides(tile)[:, columns - 1 : columns], rows - 1 - row, row)
@@ -364,8 +363,10 @@
         value = value - jnp.where(lane == columns - 1, edge, 0.0)
         value = value - jnp.where(row == rows - 1, end, 0.0)
         value = jnp.where(wet, value, 0.0)
-        residual_ref[tile] = value
+        field_ref[pl.ds(first_row(tile), rows), :] = value
         return carry
+
+    over_tiles(weights, 0)
 
     def all_of(total):
         return jnp.sum(total, keepdims=True)
@@ -374,7 +375,9 @@
 
     def apply(base, step, rolled, totals):
         tile = shift(base, step)
-        own, east, west, north, south, side, side_turned, ends = neighbours(base, step, rolled)
+        own, east, west, north, south, side, side_turned, ends = neighbours(
+            base, step, rolled, field_ref
+        )
         others = (
             (east_ref[tile] * east + west_ref[tile] * west)
             + (north_ref[tile] * north + south_ref[tile] * south)
@@ -388,14 +391,6 @@
     def sums():
         squares, products = over_tiles(apply, (zero, zero))
         return all_of(squares), all_of(products)
-
-    def copy_back(base, step, rolled, carry):
-        tile = shift(base, step)
-        field_ref[pl.ds(first_row(tile), rows), :] = residual_ref[tile]
-        return carry
-
-    over_tiles(begin, 0)
-    over_tiles(copy_back, 0)
 
     norm, product = sums()
     size = norm / product
@@ -412,13 +407,14 @@
     over_tiles(first, 0)
 
     def next_sizes(state):
-        norm, size = state
-        later, product = sums()
-        ratio = later / norm
-        return later, ratio, later / (product - ratio * (later / size))
+        inverse, last = state
+        norm, product = sums()
+        ratio = norm * inverse
+        product = product - ratio * ratio * last
+        return norm, product, ratio, norm / product
 
     def middle(_, state):
-        later, ratio, size = next_sizes(state)
+        norm, product, ratio, size = next_sizes(state)
 
         def advance(base, step, rolled, carry):
             tile = shift(base, step)
@@ -432,10 +428,10 @@
             return carry
 
         over_tiles(advance, 0)
-        return later, size
-
-    state = lax.fori_loop(1, ITERS - 1, middle, (norm, size))
-    _, ratio, last_size = next_sizes(state)
+        return 1.0 / norm, product
+
+    state = lax.fori_loop(1, ITERS - 1, middle, (1.0 / norm, product))
+    _, _, ratio, last_size = next_sizes(state)
 
     def finish(base, step, rolled, carry):
         tile = shift(base, step)
@@ -462,6 +458,7 @@
 def cg_of(got, thickness, rows):
     tiles, columns = got.shape[0], got.shape[-1]
     field = pltpu.VMEM((tiles, rows, columns), jnp.float32)
+    padded = pltpu.VMEM((tiles * rows + 16, columns), jnp.float32)
     return pl.pallas_call(
         cg_kernel,
         in_specs=[
@@ -470,7 +467,7 @@
         ],
         out_specs=pl.BlockSpec(memory_space=pltpu.VMEM),
         out_shape=jax.ShapeDtypeStruct(got.shape, jnp.int32),
-        scratch_shapes=[pltpu.VMEM((tiles * rows + 16, columns), jnp.float32)] + [field] * 13,
+        scratch_shapes=[padded] + [field] * 12 + [padded],
         compiler_params=pltpu.CompilerParams(
             vmem_limit_bytes=(4 << 20) + 18 * tiles * rows * columns * 4
         ),

time: 44.6 us -> 45 us (level)
    pallas_call x1, Pallas kernels: 3.41 us -> 3.94 us  [message_of(): pl.pallas_call(message_kernel, in_specs=[pl.BlockSpec(memory_space=pltpu....]
where the time goes in v5:
time: 45 us; the launch traced here: 44.8 us
  blocking collectives  33.5 us (74%)
  Pallas kernels  10.6 us (24%)
  between operations  0.65 us (1%)
    all_to_all x1, blocking collectives, on_device(): lax.all_to_all(message, 'tile', split_axis=0, concat_axis=0, tiled=True)  19.3 us
    all_to_all x1, blocking collectives, on_device(): home = lax.all_to_all(back, 'tile', split_axis=0, concat_axis=0, tiled=True)  14.2 us
    pallas_call x1, Pallas kernels, cg_of(): pl.pallas_call(cg_kernel, in_specs=[pl.BlockSpec(memory_space=pltpu.SMEM)...  5.64 us
    pallas_call x1, Pallas kernels, message_of(): pl.pallas_call(message_kernel, in_specs=[pl.BlockSpec(memory_space=pltpu....  3.94 us
    pallas_call x1, Pallas kernels, home_of(): pl.pallas_call(home_kernel, grid=(members // step,), in_specs=[pl.BlockSp...  0.99 us

profile of v5, /device:TPU:0, one launch (start us, length us, event | category | flops | bytes accessed | tf_op | source)
XLA Modules:
  0.0 44.8 jit_solution(11713281427256538543)
XLA Ops:
  0.6 3.9 %shard_map.77 = s32[32,5,4,128]{3,2,1,0:T(4,128)} custom-call(f32[8]{0:T(128)} %thickness_ref.3, s32[1,4]{1,0:T(1,128)} %codes_ref.1, bf16[32,8,16,128]{3,2,1,0:T(8,128)(2,1)} %zonal_hbm.1, bf16[32,8,16,128]{3,2,1,0:T(8,128)(2,1)} %meridional_hbm.1, bf16[8,16,128]{2,1,0:T(8,128)(2,1)} %fraction_hbm.1, s32[16,128]{1,0:T(8,128)} %land_hbm.1), custom_call_target="tpu_custom_call" | custom-call | tf_op jit(solution)/shard_map/pallas_call | solution.py:186
  4.6 0.0 copy-start
  4.6 19.3 %all_to_all.10.got_ref = s32[32,5,4,128]{3,2,1,0:T(4,128)S(1)} all-to-all(s32[32,5,4,128]{3,2,1,0:T(4,128)} %shard_map.77), channel_id=1, replica_groups=mesh['tile'=32] {'tile'}, dimensions={0} | all-to-all | bytes 655360 | tf_op jit(solution)/shard_map/all_to_all | solution.py:508
  23.9 0.0 copy-done
  23.9 5.6 %shard_map.78 = s32[32,5,4,128]{3,2,1,0:T(4,128)S(1)} custom-call(f32[8]{0:T(128)S(1)} %copy-done, s32[32,5,4,128]{3,2,1,0:T(4,128)S(1)} %all_to_all.10.got_ref), custom_call_target="tpu_custom_call" | custom-call | tf_op jit(solution)/shard_map/pallas_call | solution.py:462
  29.5 14.2 %all_to_all.11.home_ref = s32[32,5,4,128]{3,2,1,0:T(4,128)S(1)} all-to-all(s32[32,5,4,128]{3,2,1,0:T(4,128)S(1)} %shard_map.78), channel_id=1, replica_groups=mesh['tile'=32] {'tile'}, dimensions={0} | all-to-all | bytes 655360 | tf_op jit(solution)/shard_map/all_to_all | solution.py:510
  43.8 1.0 %shard_map.79 = (f32[32,16,128]{2,1,0:T(8,128)}, f32[32,16,128]{2,1,0:T(8,128)}) custom-call(s32[32,5,4,128]{3,2,1,0:T(4,128)S(1)} %all_to_all.11.home_ref), custom_call_target="tpu_custom_call" | custom-call | tf_op jit(solution)/shard_map/pallas_call | solution.py:492
Async XLA Ops:
  4.6 19.3 %copy-start = (f32[8]{0:T(128)S(1)}, f32[8]{0:T(128)}, u32[]{:S(2)}) copy-start(f32[8]{0:T(128)} %thickness_ref.3) | copy-start | bytes 100

commit v6 on v5

--- a/solution.py
+++ b/solution.py
@@ -182,7 +182,7 @@
 
 def message_of(zonal, meridional, fraction, thickness, land_mask, codes):
     members, _, _, columns = zonal.shape
-    group = 4 if members % 4 == 0 else 1
+    group = 16 if members % 16 == 0 else 1
     return pl.pallas_call(
         message_kernel,
         in_specs=[pl.BlockSpec(memory_space=pltpu.SMEM)] * 2

time: 45 us -> 44.5 us (0.989)
  Pallas kernels: 10.6 us -> 10.1 us
    pallas_call x1, Pallas kernels: 3.94 us -> 3.48 us  [message_of(): pl.pallas_call(message_kernel, in_specs=[pl.BlockSpec(memory_space=pltpu....]
where the time goes in v6:
time: 44.5 us; the launch traced here: 44.3 us
  blocking collectives  33.5 us (75%)
  Pallas kernels  10.1 us (23%)
  between operations  0.65 us (1%)
    all_to_all x1, blocking collectives, on_device(): lax.all_to_all(message, 'tile', split_axis=0, concat_axis=0, tiled=True)  19.3 us
    all_to_all x1, blocking collectives, on_device(): home = lax.all_to_all(back, 'tile', split_axis=0, concat_axis=0, tiled=True)  14.2 us
    pallas_call x1, Pallas kernels, cg_of(): pl.pallas_call(cg_kernel, in_specs=[pl.BlockSpec(memory_space=pltpu.SMEM)...  5.64 us
    pallas_call x1, Pallas kernels, message_of(): pl.pallas_call(message_kernel, in_specs=[pl.BlockSpec(memory_space=pltpu....  3.48 us
    pallas_call x1, Pallas kernels, home_of(): pl.pallas_call(home_kernel, grid=(members // step,), in_specs=[pl.BlockSp...  0.99 us

profile of v6, /device:TPU:0, one launch (start us, length us, event | category | flops | bytes accessed | tf_op | source)
XLA Modules:
  0.0 44.3 jit_solution(7172286329730523595)
XLA Ops:
  0.6 3.5 %shard_map.77 = s32[32,5,4,128]{3,2,1,0:T(4,128)} custom-call(f32[8]{0:T(128)} %thickness_ref.3, s32[1,4]{1,0:T(1,128)} %codes_ref.1, bf16[32,8,16,128]{3,2,1,0:T(8,128)(2,1)} %zonal_hbm.1, bf16[32,8,16,128]{3,2,1,0:T(8,128)(2,1)} %meridional_hbm.1, bf16[8,16,128]{2,1,0:T(8,128)(2,1)} %fraction_hbm.1, s32[16,128]{1,0:T(8,128)} %land_hbm.1), custom_call_target="tpu_custom_call" | custom-call | tf_op jit(solution)/shard_map/pallas_call | solution.py:186
  4.1 0.0 copy-start
  4.1 19.3 %all_to_all.10.got_ref = s32[32,5,4,128]{3,2,1,0:T(4,128)S(1)} all-to-all(s32[32,5,4,128]{3,2,1,0:T(4,128)} %shard_map.77), channel_id=1, replica_groups=mesh['tile'=32] {'tile'}, dimensions={0} | all-to-all | bytes 655360 | tf_op jit(solution)/shard_map/all_to_all | solution.py:508
  23.4 0.0 copy-done
  23.4 5.6 %shard_map.78 = s32[32,5,4,128]{3,2,1,0:T(4,128)S(1)} custom-call(f32[8]{0:T(128)S(1)} %copy-done, s32[32,5,4,128]{3,2,1,0:T(4,128)S(1)} %all_to_all.10.got_ref), custom_call_target="tpu_custom_call" | custom-call | tf_op jit(solution)/shard_map/pallas_call | solution.py:462
  29.1 14.2 %all_to_all.11.home_ref = s32[32,5,4,128]{3,2,1,0:T(4,128)S(1)} all-to-all(s32[32,5,4,128]{3,2,1,0:T(4,128)S(1)} %shard_map.78), channel_id=1, replica_groups=mesh['tile'=32] {'tile'}, dimensions={0} | all-to-all | bytes 655360 | tf_op jit(solution)/shard_map/all_to_all | solution.py:510
  43.3 1.0 %shard_map.79 = (f32[32,16,128]{2,1,0:T(8,128)}, f32[32,16,128]{2,1,0:T(8,128)}) custom-call(s32[32,5,4,128]{3,2,1,0:T(4,128)S(1)} %all_to_all.11.home_ref), custom_call_target="tpu_custom_call" | custom-call | tf_op jit(solution)/shard_map/pallas_call | solution.py:492
Async XLA Ops:
  4.1 19.3 %copy-start = (f32[8]{0:T(128)S(1)}, f32[8]{0:T(128)}, u32[]{:S(2)}) copy-start(f32[8]{0:T(128)} %thickness_ref.3) | copy-start | bytes 100

commit v7 on v6

--- a/solution.py
+++ b/solution.py
@@ -80,13 +80,16 @@
 
 
 def message_kernel(
-    thickness_ref,
-    codes_ref,
+    group,
+    thickness_hbm,
+    codes_hbm,
     zonal_hbm,
     meridional_hbm,
     fraction_hbm,
     land_hbm,
     out_hbm,
+    thickness_ref,
+    codes_ref,
     zonal_ref,
     meridional_ref,
     fraction_ref,
@@ -96,7 +99,6 @@
     out_sems,
 ):
     members, levels, rows, columns = zonal_ref.shape
-    group = members // out_sems.shape[0]
 
     def copies_in(at):
         part = pl.ds(at * group, group)
@@ -111,15 +113,24 @@
         part = pl.ds(at * group, group)
         return pltpu.make_async_copy(out_ref.at[part], out_hbm.at[part], out_sems.at[at])
 
-    land_copy = pltpu.make_async_copy(land_hbm, land_ref, in_sems.at[2, 0])
-    fraction_copy = pltpu.make_async_copy(fraction_hbm, fraction_ref, in_sems.at[2, 1])
-    fraction_copy.start()
-    land_copy.start()
+    small = [
+        pltpu.make_async_copy(source, target, in_sems.at[2, at])
+        for at, (source, target) in enumerate(
+            (
+                (fraction_hbm, fraction_ref),
+                (thickness_hbm, thickness_ref),
+                (land_hbm, land_ref),
+                (codes_hbm, codes_ref),
+            )
+        )
+    ]
+    for copy in small:
+        copy.start()
     for at in range(members // group):
         for copy in copies_in(at):
             copy.start()
-    fraction_copy.wait()
-    land_copy.wait()
+    for copy in small:
+        copy.wait()
     lane = lax.broadcasted_iota(jnp.int32, (rows, columns), 1)
     row = lax.broadcasted_iota(jnp.int32, (rows, columns), 0)
     place = lax.broadcasted_iota(jnp.int32, (8, columns), 0)
@@ -182,20 +193,21 @@
 
 def message_of(zonal, meridional, fraction, thickness, land_mask, codes):
     members, _, _, columns = zonal.shape
-    group = 16 if members % 16 == 0 else 1
+    group = 8 if members % 8 == 0 else 1
     return pl.pallas_call(
-        message_kernel,
-        in_specs=[pl.BlockSpec(memory_space=pltpu.SMEM)] * 2
-        + [pl.BlockSpec(memory_space=pl.ANY)] * 4,
+        functools.partial(message_kernel, group),
+        in_specs=[pl.BlockSpec(memory_space=pl.ANY)] * 6,
         out_specs=pl.BlockSpec(memory_space=pl.ANY),
         out_shape=jax.ShapeDtypeStruct((members, PIECES, 4, columns), jnp.int32),
         scratch_shapes=[
+            pltpu.SMEM(thickness.shape, thickness.dtype),
+            pltpu.SMEM(codes.shape, codes.dtype),
             pltpu.VMEM(zonal.shape, zonal.dtype),
             pltpu.VMEM(meridional.shape, meridional.dtype),
             pltpu.VMEM(fraction.shape, fraction.dtype),
             pltpu.VMEM(land_mask.shape, land_mask.dtype),
             pltpu.VMEM((members, PIECES, 4, columns), jnp.int32),
-            pltpu.SemaphoreType.DMA((3, max(2, members // group))),
+            pltpu.SemaphoreType.DMA((3, max(4, members // group))),
             pltpu.SemaphoreType.DMA((members // group,)),
         ],
         compiler_params=pltpu.CompilerParams(vmem_limit_bytes=60 << 20),
@@ -221,7 +233,7 @@
 
 
 def cg_kernel(
-    thickness_ref,
+    thickness_hbm,
     got_ref,
     out_ref,
     field_ref,
@@ -238,6 +250,8 @@
     ends_ref,
     surface_ref,
     root_ref,
+    thickness_ref,
+    thickness_sem,
 ):
     tiles, rows, columns = image_ref.shape
     levels = thickness_ref.shape[0]
@@ -304,7 +318,8 @@
         north, south = field(tile, 1, ref), field(tile, -1, ref)
         return own, east, west, north, south, side, reversed_rows(side), ends
 
-    levels_sum = sum_of(thickness_ref, levels)
+    thickness_copy = pltpu.make_async_copy(thickness_hbm, thickness_ref, thickness_sem)
+    thickness_copy.start()
     padding = jnp.zeros((8, columns), jnp.float32)
     for ref in (field_ref, root_ref):
         ref[0:8, :] = padding
@@ -318,6 +333,8 @@
         return carry
 
     over_tiles(read_depth, 0)
+    thickness_copy.wait()
+    levels_sum = sum_of(thickness_ref, levels)
 
     def weights(base, step, rolled, carry):
         tile = shift(base, step)
@@ -462,12 +479,14 @@
     return pl.pallas_call(
         cg_kernel,
         in_specs=[
-            pl.BlockSpec(memory_space=pltpu.SMEM),
+            pl.BlockSpec(memory_space=pl.ANY),
             pl.BlockSpec(memory_space=pltpu.VMEM),
         ],
         out_specs=pl.BlockSpec(memory_space=pltpu.VMEM),
         out_shape=jax.ShapeDtypeStruct(got.shape, jnp.int32),
-        scratch_shapes=[padded] + [field] * 12 + [padded],
+        scratch_shapes=[padded]
+        + [field] * 12
+        + [padded, pltpu.SMEM(thickness.shape, thickness.dtype), pltpu.SemaphoreType.DMA],
         compiler_params=pltpu.CompilerParams(
             vmem_limit_bytes=(4 << 20) + 18 * tiles * rows * columns * 4
         ),

time: 44.5 us -> 43.8 us (0.984)
  Pallas kernels: 10.1 us -> 9.38 us
    pallas_call x2, Pallas kernels: 9.12 us -> 8.39 us  [the longest x1 5.65 us: cg_of(): pl.pallas_call(cg_kernel, in_specs=[pl.BlockSpec(memory_space=pl.ANY), pl...]
where the time goes in v7:
time: 43.8 us; the launch traced here: 43.6 us
  blocking collectives  33.5 us (76%)
  Pallas kernels  9.38 us (21%)
  between operations  0.66 us (2%)
    all_to_all x1, blocking collectives, on_device(): lax.all_to_all(message, 'tile', split_axis=0, concat_axis=0, tiled=True)  19.3 us
    all_to_all x1, blocking collectives, on_device(): home = lax.all_to_all(back, 'tile', split_axis=0, concat_axis=0, tiled=True)  14.2 us
    pallas_call x1, Pallas kernels, cg_of(): pl.pallas_call(cg_kernel, in_specs=[pl.BlockSpec(memory_space=pl.ANY), pl...  5.65 us
    pallas_call x1, Pallas kernels, message_of(): pl.pallas_call(functools.partial(message_kernel, group), in_specs=[pl.Blo...  2.74 us
    pallas_call x1, Pallas kernels, home_of(): pl.pallas_call(home_kernel, grid=(members // step,), in_specs=[pl.BlockSp...  0.99 us

profile of v7, /device:TPU:0, one launch (start us, length us, event | category | flops | bytes accessed | tf_op | source)
XLA Modules:
  0.0 43.6 jit_solution(7960907184394564257)
XLA Ops:
  0.6 2.7 %shard_map.77 = s32[32,5,4,128]{3,2,1,0:T(4,128)} custom-call(f32[8]{0:T(128)} %thickness_hbm.3, s32[1,4]{1,0:T(1,128)} %codes_hbm.1, bf16[32,8,16,128]{3,2,1,0:T(8,128)(2,1)} %zonal_hbm.1, bf16[32,8,16,128]{3,2,1,0:T(8,128)(2,1)} %meridional_hbm.1, bf16[8,16,128]{2,1,0:T(8,128)(2,1)} %fraction_hbm.1, s32[16,128]{1,0:T(8,128)} %land_hbm.1), custom_call_target="tpu_custom_call" | custom-call | tf_op jit(solution)/shard_map/pallas_call | solution.py:197
  3.4 0.0 copy-start
  3.4 19.3 %all_to_all.10.got_ref = s32[32,5,4,128]{3,2,1,0:T(4,128)S(1)} all-to-all(s32[32,5,4,128]{3,2,1,0:T(4,128)} %shard_map.77), channel_id=1, replica_groups=mesh['tile'=32] {'tile'}, dimensions={0} | all-to-all | bytes 655360 | tf_op jit(solution)/shard_map/all_to_all | solution.py:527
  22.7 0.0 copy-done
  22.7 5.7 %shard_map.78 = s32[32,5,4,128]{3,2,1,0:T(4,128)S(1)} custom-call(f32[8]{0:T(128)S(1)} %copy-done, s32[32,5,4,128]{3,2,1,0:T(4,128)S(1)} %all_to_all.10.got_ref), custom_call_target="tpu_custom_call" | custom-call | tf_op jit(solution)/shard_map/pallas_call | solution.py:479
  28.4 14.2 %all_to_all.11.home_ref = s32[32,5,4,128]{3,2,1,0:T(4,128)S(1)} all-to-all(s32[32,5,4,128]{3,2,1,0:T(4,128)S(1)} %shard_map.78), channel_id=1, replica_groups=mesh['tile'=32] {'tile'}, dimensions={0} | all-to-all | bytes 655360 | tf_op jit(solution)/shard_map/all_to_all | solution.py:529
  42.6 1.0 %shard_map.79 = (f32[32,16,128]{2,1,0:T(8,128)}, f32[32,16,128]{2,1,0:T(8,128)}) custom-call(s32[32,5,4,128]{3,2,1,0:T(4,128)S(1)} %all_to_all.11.home_ref), custom_call_target="tpu_custom_call" | custom-call | tf_op jit(solution)/shard_map/pallas_call | solution.py:511
Async XLA Ops:
  3.4 19.3 %copy-start = (f32[8]{0:T(128)S(1)}, f32[8]{0:T(128)}, u32[]{:S(2)}) copy-start(f32[8]{0:T(128)} %thickness_hbm.3) | copy-start | bytes 100

commit v8 on v7

--- a/solution.py
+++ b/solution.py
@@ -506,7 +506,7 @@
 
 def home_of(home, members, rows):
     columns = home.shape[-1]
-    step = 16 if members % 16 == 0 else 1
+    step = 32 if members % 32 == 0 else 1
     result = jax.ShapeDtypeStruct((members, rows, columns), jnp.float32)
     return pl.pallas_call(
         home_kernel,

time: 43.8 us -> 43.9 us (level)
  no operation moved by 1% of the time
where the time goes in v8:
time: 43.9 us; the launch traced here: 43.6 us
  blocking collectives  33.5 us (76%)
  Pallas kernels  9.44 us (22%)
  between operations  0.66 us (2%)
    all_to_all x1, blocking collectives, on_device(): lax.all_to_all(message, 'tile', split_axis=0, concat_axis=0, tiled=True)  19.3 us
    all_to_all x1, blocking collectives, on_device(): home = lax.all_to_all(back, 'tile', split_axis=0, concat_axis=0, tiled=True)  14.2 us
    pallas_call x1, Pallas kernels, cg_of(): pl.pallas_call(cg_kernel, in_specs=[pl.BlockSpec(memory_space=pl.ANY), pl...  5.65 us
    pallas_call x1, Pallas kernels, message_of(): pl.pallas_call(functools.partial(message_kernel, group), in_specs=[pl.Blo...  2.74 us
    pallas_call x1, Pallas kernels, home_of(): pl.pallas_call(home_kernel, grid=(members // step,), in_specs=[pl.BlockSp...  1.05 us

profile of v8, /device:TPU:0, one launch (start us, length us, event | category | flops | bytes accessed | tf_op | source)
XLA Modules:
  0.0 43.6 jit_solution(13148664959109907622)
XLA Ops:
  0.6 2.7 %shard_map.77 = s32[32,5,4,128]{3,2,1,0:T(4,128)} custom-call(f32[8]{0:T(128)} %thickness_hbm.3, s32[1,4]{1,0:T(1,128)} %codes_hbm.1, bf16[32,8,16,128]{3,2,1,0:T(8,128)(2,1)} %zonal_hbm.1, bf16[32,8,16,128]{3,2,1,0:T(8,128)(2,1)} %meridional_hbm.1, bf16[8,16,128]{2,1,0:T(8,128)(2,1)} %fraction_hbm.1, s32[16,128]{1,0:T(8,128)} %land_hbm.1), custom_call_target="tpu_custom_call" | custom-call | tf_op jit(solution)/shard_map/pallas_call | solution.py:197
  3.4 0.0 copy-start
  3.4 19.3 %all_to_all.10.got_ref = s32[32,5,4,128]{3,2,1,0:T(4,128)S(1)} all-to-all(s32[32,5,4,128]{3,2,1,0:T(4,128)} %shard_map.77), channel_id=1, replica_groups=mesh['tile'=32] {'tile'}, dimensions={0} | all-to-all | bytes 655360 | tf_op jit(solution)/shard_map/all_to_all | solution.py:527
  22.7 0.0 copy-done
  22.7 5.7 %shard_map.78 = s32[32,5,4,128]{3,2,1,0:T(4,128)S(1)} custom-call(f32[8]{0:T(128)S(1)} %copy-done, s32[32,5,4,128]{3,2,1,0:T(4,128)S(1)} %all_to_all.10.got_ref), custom_call_target="tpu_custom_call" | custom-call | tf_op jit(solution)/shard_map/pallas_call | solution.py:479
  28.4 14.2 %all_to_all.11.home_ref = s32[32,5,4,128]{3,2,1,0:T(4,128)S(1)} all-to-all(s32[32,5,4,128]{3,2,1,0:T(4,128)S(1)} %shard_map.78), channel_id=1, replica_groups=mesh['tile'=32] {'tile'}, dimensions={0} | all-to-all | bytes 655360 | tf_op jit(solution)/shard_map/all_to_all | solution.py:529
  42.6 1.1 %shard_map.79 = (f32[32,16,128]{2,1,0:T(8,128)}, f32[32,16,128]{2,1,0:T(8,128)}) custom-call(s32[32,5,4,128]{3,2,1,0:T(4,128)S(1)} %all_to_all.11.home_ref), custom_call_target="tpu_custom_call" | custom-call | tf_op jit(solution)/shard_map/pallas_call | solution.py:511
Async XLA Ops:
  3.4 19.3 %copy-start = (f32[8]{0:T(128)S(1)}, f32[8]{0:T(128)}, u32[]{:S(2)}) copy-start(f32[8]{0:T(128)} %thickness_hbm.3) | copy-start | bytes 100

commit v9 on v7

--- a/solution.py
+++ b/solution.py
@@ -179,7 +179,8 @@
         copy_out(at).start()
         return carry
 
-    lax.fori_loop(0, members // group, some, 0)
+    for at in range(members // group):
+        some(at, 0)
     for at in range(members // group):
         copy_out(at).wait()
 

time: 43.8 us -> 43.8 us (level)
  no operation moved by 1% of the time
where the time goes in v9:
time: 43.8 us; the launch traced here: 43.6 us
  blocking collectives  33.5 us (76%)
  Pallas kernels  9.4 us (21%)
  between operations  0.66 us (2%)
    all_to_all x1, blocking collectives, on_device(): lax.all_to_all(message, 'tile', split_axis=0, concat_axis=0, tiled=True)  19.3 us
    all_to_all x1, blocking collectives, on_device(): home = lax.all_to_all(back, 'tile', split_axis=0, concat_axis=0, tiled=True)  14.2 us
    pallas_call x1, Pallas kernels, cg_of(): pl.pallas_call(cg_kernel, in_specs=[pl.BlockSpec(memory_space=pl.ANY), pl...  5.65 us
    pallas_call x1, Pallas kernels, message_of(): pl.pallas_call(functools.partial(message_kernel, group), in_specs=[pl.Blo...  2.76 us
    pallas_call x1, Pallas kernels, home_of(): pl.pallas_call(home_kernel, grid=(members // step,), in_specs=[pl.BlockSp...  0.99 us

profile of v9, /device:TPU:0, one launch (start us, length us, event | category | flops | bytes accessed | tf_op | source)
XLA Modules:
  0.0 43.6 jit_solution(14443285868936114660)
XLA Ops:
  0.6 2.8 %shard_map.77 = s32[32,5,4,128]{3,2,1,0:T(4,128)} custom-call(f32[8]{0:T(128)} %thickness_hbm.3, s32[1,4]{1,0:T(1,128)} %codes_hbm.1, bf16[32,8,16,128]{3,2,1,0:T(8,128)(2,1)} %zonal_hbm.1, bf16[32,8,16,128]{3,2,1,0:T(8,128)(2,1)} %meridional_hbm.1, bf16[8,16,128]{2,1,0:T(8,128)(2,1)} %fraction_hbm.1, s32[16,128]{1,0:T(8,128)} %land_hbm.1), custom_call_target="tpu_custom_call" | custom-call | tf_op jit(solution)/shard_map/pallas_call | solution.py:198
  3.4 0.0 copy-start
  3.4 19.3 %all_to_all.10.got_ref = s32[32,5,4,128]{3,2,1,0:T(4,128)S(1)} all-to-all(s32[32,5,4,128]{3,2,1,0:T(4,128)} %shard_map.77), channel_id=1, replica_groups=mesh['tile'=32] {'tile'}, dimensions={0} | all-to-all | bytes 655360 | tf_op jit(solution)/shard_map/all_to_all | solution.py:528
  22.7 0.0 copy-done
  22.7 5.7 %shard_map.78 = s32[32,5,4,128]{3,2,1,0:T(4,128)S(1)} custom-call(f32[8]{0:T(128)S(1)} %copy-done, s32[32,5,4,128]{3,2,1,0:T(4,128)S(1)} %all_to_all.10.got_ref), custom_call_target="tpu_custom_call" | custom-call | tf_op jit(solution)/shard_map/pallas_call | solution.py:480
  28.4 14.2 %all_to_all.11.home_ref = s32[32,5,4,128]{3,2,1,0:T(4,128)S(1)} all-to-all(s32[32,5,4,128]{3,2,1,0:T(4,128)S(1)} %shard_map.78), channel_id=1, replica_groups=mesh['tile'=32] {'tile'}, dimensions={0} | all-to-all | bytes 655360 | tf_op jit(solution)/shard_map/all_to_all | solution.py:530
  42.6 1.0 %shard_map.79 = (f32[32,16,128]{2,1,0:T(8,128)}, f32[32,16,128]{2,1,0:T(8,128)}) custom-call(s32[32,5,4,128]{3,2,1,0:T(4,128)S(1)} %all_to_all.11.home_ref), custom_call_target="tpu_custom_call" | custom-call | tf_op jit(solution)/shard_map/pallas_call | solution.py:512
Async XLA Ops:
  3.4 19.3 %copy-start = (f32[8]{0:T(128)S(1)}, f32[8]{0:T(128)}, u32[]{:S(2)}) copy-start(f32[8]{0:T(128)} %thickness_hbm.3) | copy-start | bytes 100
